TPU v7x, 128 devices: a whole 4x4x4 slice. The times are simulated.
128 devices in a mesh: section: 4 (over y_lo, core), row: 4 (over x), col: 8 (over y_hi, z).
Axes of the slice: x: 4, y: 4 (y_hi: 2, y_lo: 2; y = y_hi * 2 + y_lo), z: 4, core: 2. Of those that a mesh axis runs over, the one named last changes fastest.
Arguments:
- inputs: bfloat16 [4, 1024, 6144], P('section', 'col', 'row'), may hold values from -450 to 450
- cotangent: bfloat16 [4, 1024, 6144], P('section', 'col', 'row'), may hold values from -2 to 2
- stashed: bfloat16 [4, 1024, 12288], P('section', 'row', 'col'), may hold values from -6 to 6
- weight_in: bfloat16 [4, 6144, 12288], P('section', 'row', 'col'), may hold values from -0.078125 to 0.078125
- weight_out: bfloat16 [4, 12288, 6144], P('section', 'col', 'row'), may hold values from -0.0546875 to 0.0546875
- norm_gain: float32 [4, 6144], P('section', 'row'), may hold values from 0.3 to 8
Outputs:
- grad_in: bfloat16 [4, 6144, 12288], P('section', 'row', 'col')
- grad_out: bfloat16 [4, 12288, 6144], P('section', 'col', 'row')
- grad_gain: float32 [4, 6144], P('section', 'row')
- passed: bfloat16 [4, 1024, 6144], P('section', 'col', 'row')
All inputs are finite; a program needn't handle non-finite values.
Results may differ from a plain program's by a relative error of at most 0.0015.
The roundings to bfloat16 on the way count: a program that leaves them out, or rounds other values in their place, can miss the bound.
Values may be sent and summed in bfloat16 or wider, within the bound.
No kernel may reach another device: no remote copies, remote signals or barrier semaphores. Data moves between devices by JAX's collectives and lax.ppermute only.
A program may use at most 128 MiB of HBM per device.

v0:
```python
import jax
import jax.numpy as jnp
from jax import lax
from jax.sharding import PartitionSpec as P

epsilon = 1e-06
half_root = 0.7071067811865476
density_factor = 0.3989422804014327


def passed_along(block, axis, distance):
    devices = range(lax.axis_size(axis))
    route = [(i - distance, i) for i in devices if i - distance in devices]
    return lax.ppermute(block, axis, route)


def gelu_parts(values):
    cumulative = 0.5 * (1.0 + lax.erf(values * half_root))
    density = jnp.exp(-0.5 * values * values) * density_factor
    return (values * cumulative, cumulative + values * density)


def times_trans(left, right):
    return lax.dot_general(
        left, right, (((1,), (1,)), ((), ())), preferred_element_type=jnp.float32
    )


def trans_times(left, right):
    return lax.dot_general(
        left, right, (((0,), (0,)), ((), ())), preferred_element_type=jnp.float32
    )


def local(inputs, cotangent, stashed, weight_in, weight_out, norm_gain):
    local_input = inputs[0]
    upstream = cotangent[0]
    hidden_pre = stashed[0]
    first_weight = weight_in[0]
    second_weight = weight_out[0]
    gains = norm_gain[0]
    feature_count = gains.shape[0] * lax.axis_size("row")
    grad_full = lax.all_gather(upstream, "col", axis=0, tiled=True)
    values = local_input.astype(jnp.float32)
    totals, squares = lax.psum((jnp.sum(values, axis=1), jnp.sum(values * values, axis=1)), "row")
    average = totals / feature_count
    inv_scale = lax.rsqrt(squares / feature_count - average * average + epsilon)
    standard = (values - average[:, None]) * inv_scale[:, None]
    normed = (standard * gains).astype(jnp.bfloat16)
    normed_full = lax.all_gather(normed, "col", axis=0, tiled=True)
    activated, slopes = gelu_parts(hidden_pre.astype(jnp.float32))
    activ_full = lax.all_gather(activated.astype(jnp.bfloat16), "row", axis=0, tiled=True)
    hidden_grad = lax.psum_scatter(
        times_trans(grad_full, second_weight), "row", scatter_dimension=0, tiled=True
    )
    deltas = (hidden_grad * slopes).astype(jnp.bfloat16)
    delta_full = lax.all_gather(deltas, "row", axis=0, tiled=True)
    out_grad = trans_times(activ_full, grad_full).astype(jnp.bfloat16)
    in_grad = trans_times(normed_full, delta_full).astype(jnp.bfloat16)
    normed_grad = lax.psum_scatter(
        times_trans(delta_full, first_weight), "col", scatter_dimension=0, tiled=True
    )
    gain_grad = lax.psum(jnp.sum(normed_grad * standard, axis=0), "col")
    scaled_grad = normed_grad * gains
    first_sum, second_sum = lax.psum(
        (jnp.sum(scaled_grad, axis=1), jnp.sum(scaled_grad * standard, axis=1)), "row"
    )
    first_mean = first_sum / feature_count
    second_mean = second_sum / feature_count
    result_grad = upstream.astype(jnp.float32) + inv_scale[:, None] * (
        scaled_grad - first_mean[:, None] - standard * second_mean[:, None]
    )
    received = passed_along(result_grad.astype(jnp.bfloat16), "section", -1)
    return (in_grad[None], out_grad[None], gain_grad[None], received[None])


def solution(mesh):
    return jax.shard_map(
        local,
        mesh=mesh,
        in_specs=(
            P("section", "col", "row"),
            P("section", "col", "row"),
            P("section", "row", "col"),
            P("section", "row", "col"),
            P("section", "col", "row"),
            P("section", "row"),
        ),
        out_specs=(
            P("section", "row", "col"),
            P("section", "col", "row"),
            P("section", "row"),
            P("section", "col", "row"),
        ),
        check_vma=False,
    )
```

profile of v0, /device:TPU:1, one launch (start us, length us, event | category | flops | bytes accessed | tf_op | source)
XLA Modules:
  0.0 421.5 jit_solution(5497544873123259494)
XLA Ops:
  7.2 0.7 all-gather.12.cloned.1.call-update
  7.9 68.0 %all-gather.12.cloned.1.call-done = bf16[1,1024,1536]{2,1,0:T(8,128)(2,1)} async-done(((bf16[1,128,1536]{2,1,0:T(8,128)(2,1)}), bf16[1,1024,1536]{2,1,0:T(8,128)(2,1)}) %all-gather.12.cloned.1.call-update) | async-done | bytes 3145744 | tf_op jit(solution)/shard_map/all_gather | solution.py:43
  76.0 9.8 %fusion.4 = f32[1024,1536]{1,0:T(8,128)} fusion(bf16[1,1536,1536]{2,1,0:T(8,128)(2,1)} %param.10, bf16[1,1024,1536]{2,1,0:T(8,128)(2,1)} %all-gather.12.cloned.1.call-done), kind=kOutput, calls=%fused_computation.6 | convolution fusion | flops 4831838208 | bytes 14155776 | tf_op jit(solution)/shard_map/dot_general | solution.py:24
  85.9 62.2 %reduce-scatter.3.cloned.1.call-done = f32[256,1536]{1,0:T(8,128)} async-done(((f32[1024,1536]{1,0:T(8,128)}), f32[256,1536]{1,0:T(8,128)}) %reduce-scatter.3.cloned.1.call-update) | async-done | bytes 1572880 | tf_op jit(solution)/shard_map/reduce_scatter | solution.py:53
  148.0 3.3 fusion.16
  151.4 0.0 reduce-scatter.5.cloned.1.call-start
  151.4 39.3 %all-gather.8.cloned.1.call-done = bf16[1024,1536]{1,0:T(8,128)(2,1)} async-done(((bf16[256,1536]{1,0:T(8,128)(2,1)}), bf16[1024,1536]{1,0:T(8,128)(2,1)}) %all-gather.8.cloned.1.call-update) | async-done | bytes 3145744 | tf_op jit(solution)/shard_map/all_gather | solution.py:57
  190.8 9.8 %fusion.2 = f32[1024,1536]{1,0:T(8,128)} fusion(bf16[1024,1536]{1,0:T(8,128)(2,1)} %all-gather.8.cloned.1.call-done, bf16[1,1536,1536]{2,1,0:T(8,128)(2,1)} %param.9), kind=kOutput, calls=%fused_computation.4 | convolution fusion | flops 4831838208 | bytes 14155776 | tf_op jit(solution)/shard_map/dot_general | solution.py:24
  200.6 0.5 all-gather.10.cloned.1.call-update
  201.3 0.3 copy-done
  201.6 0.1 convert_reduce_fusion
  201.7 0.2 fusion.31
  201.9 6.6 %all-reduce.1 = (f32[128]{0:T(128)S(1)}, f32[128]{0:T(128)S(1)}) all-reduce(f32[128]{0:T(128)S(1)} %fusion.31, f32[128]{0:T(128)S(1)} %convert_reduce_fusion), channel_id=1, replica_groups=mesh['section'=4,'row'=4,'col'=8] {'row'}, use_global_device_ids=true, to_apply=%region_3.0 | all-reduce | flops 256 | bytes 2048 | tf_op jit(solution)/shard_map/psum | solution.py:45
  208.4 90.3 %reduce-scatter.5.cloned.1.call-done = f32[128,1536]{1,0:T(8,128)} async-done(((f32[1024,1536]{1,0:T(8,128)}), f32[128,1536]{1,0:T(8,128)}) %reduce-scatter.5.cloned.1.call-update) | async-done | bytes 786448 | tf_op jit(solution)/shard_map/reduce_scatter | solution.py:60
  298.7 1.5 fusion.26
  300.2 8.4 %all-reduce = (f32[128]{0:T(128)S(1)}, f32[128]{0:T(128)S(1)}) all-reduce(f32[128]{0:T(128)S(1)} %get-tuple-element.4, f32[128]{0:T(128)S(1)} %get-tuple-element.6), channel_id=1, replica_groups=mesh['section'=4,'row'=4,'col'=8] {'row'}, use_global_device_ids=true, to_apply=%region_11.0 | all-reduce | flops 256 | bytes 2048 | tf_op jit(solution)/shard_map/psum | solution.py:65
  308.6 2.3 fusion.30
  311.0 5.1 %collective-permute-start = (bf16[128,1536]{1,0:T(8,128)(2,1)S(1)}, bf16[128,1536]{1,0:T(8,128)(2,1)S(1)}, u32[]{:S(2)}, u32[]{:S(2)}) collective-permute-start(bf16[128,1536]{1,0:T(8,128)(2,1)S(1)} %get-tuple-element.13), channel_id=1, source_target_pairs={{32,0},{64,32},{96,64},{33,1},{65,33},{97,65},{34,2},{66,34},{98,6... | collective-permute-start | bytes 1179656 | tf_op jit(solution)/shard_map/ppermute | solution.py:14
  316.1 23.1 %all-gather.10.cloned.1.call-done = bf16[1024,1536]{1,0:T(8,128)(2,1)} async-done(((bf16[256,1536]{1,0:T(8,128)(2,1)}), bf16[1024,1536]{1,0:T(8,128)(2,1)}) %all-gather.10.cloned.1.call-update) | async-done | bytes 3145744 | tf_op jit(solution)/shard_map/all_gather | solution.py:52
  339.2 9.1 %fusion.1 = bf16[1,1536,1536]{2,1,0:T(8,128)(2,1)} fusion(bf16[1024,1536]{1,0:T(8,128)(2,1)} %all-gather.10.cloned.1.call-done, bf16[1,1024,1536]{2,1,0:T(8,128)(2,1)} %all-gather.12.cloned.1.call-done), kind=kOutput, calls=%fused_computation.3 | convolution fusion | flops 4834197504 | bytes 11010048 | tf_op jit(solution)/shard_map/dot_general | solution.py:30
  348.3 21.7 %psum.37 = f32[1,1536]{1,0:T(1,128)} all-reduce(f32[1,1536]{1,0:T(1,128)S(1)} %broadcast_in_dim.19), channel_id=1, replica_groups=mesh['section'=4,'row'=4,'col'=8] {'col'}, use_global_device_ids=true, to_apply=%region_7.0 | all-reduce | flops 1536 | bytes 12288 | tf_op jit(solution)/shard_map/psum | solution.py:63
  370.0 34.7 %all-gather.6.cloned.1.call-done = bf16[1024,1536]{1,0:T(8,128)(2,1)} async-done(((bf16[128,1536]{1,0:T(8,128)(2,1)}), bf16[1024,1536]{1,0:T(8,128)(2,1)}) %all-gather.6.cloned.1.call-update) | async-done | bytes 3145744 | tf_op jit(solution)/shard_map/all_gather | solution.py:50
  404.8 9.1 %fusion = bf16[1,1536,1536]{2,1,0:T(8,128)(2,1)} fusion(bf16[1024,1536]{1,0:T(8,128)(2,1)} %all-gather.6.cloned.1.call-done, bf16[1024,1536]{1,0:T(8,128)(2,1)} %all-gather.8.cloned.1.call-done), kind=kOutput, calls=%fused_computation.2 | convolution fusion | flops 4834197504 | bytes 11010048 | tf_op jit(solution)/shard_map/dot_general | solution.py:30
  413.9 0.7 copy.11
  (21 shorter events, 0.3 us)
Async XLA Ops:
  7.2 68.8 %all-gather.12.cloned.1.call-start = ((), (), s32[]{:S(2)}) async-start(), calls=%async_computation.7 | async-start | bytes 3538944 | tf_op jit(solution)/shard_map/all_gather | solution.py:43
  7.9 140.1 %reduce-scatter.3.cloned.1.call-start = ((), (), s32[]{:S(2)}) async-start(), calls=%async_computation.3 | async-start | bytes 7864320 | tf_op jit(solution)/shard_map/reduce_scatter | solution.py:53
  85.8 62.3 %copy-start.2 = (bf16[1,256,1536]{2,1,0:T(8,128)(2,1)S(1)}, bf16[1,256,1536]{2,1,0:T(8,128)(2,1)}, u32[]{:S(2)}) copy-start(bf16[1,256,1536]{2,1,0:T(8,128)(2,1)} %param.8) | copy-start | bytes 2359300
  85.8 105.0 %all-gather.8.cloned.1.call-start = ((), (), s32[]{:S(2)}) async-start(), calls=%async_computation.4 | async-start | bytes 3932160 | tf_op jit(solution)/shard_map/all_gather | solution.py:57
  151.4 147.4 %reduce-scatter.5.cloned.1.call-start = ((), (), s32[]{:S(2)}) async-start(), calls=%async_computation.6 | async-start | bytes 7077888 | tf_op jit(solution)/shard_map/reduce_scatter | solution.py:60
  200.6 0.7 copy-start.3
  200.6 1.0 copy-start
  200.6 108.1 %copy-start.1 = (bf16[1,128,1536]{2,1,0:T(8,128)(2,1)S(1)}, bf16[1,128,1536]{2,1,0:T(8,128)(2,1)}, u32[]{:S(2)}) copy-start(bf16[1,128,1536]{2,1,0:T(8,128)(2,1)} %param.7) | copy-start | bytes 1179652
  200.6 138.6 %all-gather.10.cloned.1.call-start = ((), (), s32[]{:S(2)}) async-start(), calls=%async_computation.5 | async-start | bytes 3932160 | tf_op jit(solution)/shard_map/all_gather | solution.py:52
  201.2 203.6 %all-gather.6.cloned.1.call-start = ((), (), s32[]{:S(2)}) async-start(), calls=%async_computation.2 | async-start | bytes 3538944 | tf_op jit(solution)/shard_map/all_gather | solution.py:50
  311.0 59.0 %collective-permute-start = (bf16[128,1536]{1,0:T(8,128)(2,1)S(1)}, bf16[128,1536]{1,0:T(8,128)(2,1)S(1)}, u32[]{:S(2)}, u32[]{:S(2)}) collective-permute-start(bf16[128,1536]{1,0:T(8,128)(2,1)S(1)} %get-tuple-element.13), channel_id=1, source_target_pairs={{32,0},{64,32},{96,64},{33,1},{65,33},{97,65},{34,2},{66,34},{98,6... | collective-permute-start | bytes 1179656 | tf_op jit(solution)/shard_map/ppermute | solution.py:14
Sparse Core Ops, SparseCore 0:
  10.3 65.6 all-gather.11
  85.9 62.0 reduce-scatter.2
  151.5 39.2 all-gather.7
  200.7 97.9 reduce-scatter.4
  300.8 38.3 all-gather.9
  341.9 62.8 all-gather.5
where the time goes:
time: 422 us; the launch traced here: 421 us
  waiting for transfers between devices  319 us (76%)
  matrix products  37.9 us (9%)
  blocking collectives  36.7 us (9%)
  between operations  14.1 us (3%)
  other arithmetic  7.43 us (2%)
  starting transfers between devices  5.39 us (1%)
    reduce_scatter x1, waiting for transfers between devices, local(): lax.psum_scatter(times_trans(delta_full, first_weight), 'col', scatter_di...  90.3 us
    all_gather x1, waiting for transfers between devices, local(): grad_full = lax.all_gather(upstream, 'col', axis=0, tiled=True)  68 us
    reduce_scatter x1, waiting for transfers between devices, local(): lax.psum_scatter(times_trans(grad_full, second_weight), 'row', scatter_di...  62.2 us
    all_gather x1, waiting for transfers between devices, local(): delta_full = lax.all_gather(deltas, 'row', axis=0, tiled=True)  39.3 us
    all_gather x1, waiting for transfers between devices, local(): normed_full = lax.all_gather(normed, 'col', axis=0, tiled=True)  34.7 us
    all_gather x1, waiting for transfers between devices, local(): lax.all_gather(activated.astype(jnp.bfloat16), 'row', axis=0, tiled=True)  23.1 us
    psum x1, blocking collectives, local(): gain_grad = lax.psum(jnp.sum(normed_grad * standard, axis=0), 'col')  21.7 us
    dot_general x2, matrix products, times_trans(): lax.dot_general(left, right, (((1,), (1,)), ((), ())), preferred_element_...  19.6 us
  transfers between devices with their start and end apart: 7, of which 6 were waited for; matrix products, arithmetic and copies ran while one was open for 3% of the time, Pallas kernels for 0%

commit v1 on v0

v1 whole, which is shorter than its diff:
```python
import functools

import jax
import jax.numpy as jnp
from jax import lax
from jax.experimental import pallas as pl
from jax.experimental.pallas import tpu as pltpu
from jax.sharding import PartitionSpec as P

epsilon = 1e-06
half_root = 0.7071067811865476
density_factor = 0.3989422804014327

chunk_rows = (64, 64)
vmem_bytes = 40 * 1024 * 1024


def along_x(block, step):
    return lax.ppermute(block, "row", [(i, (i + step) % 4) for i in range(4)])


def along_z(block, step):
    route = [(j, j // 4 * 4 + (j % 4 + step) % 4) for j in range(8)]
    return lax.ppermute(block, "col", route)


def along_y(block):
    return lax.ppermute(block, "col", [(j, (j + 4) % 8) for j in range(8)])


def to_layer_before(block):
    return lax.ppermute(block, "section", [(i, i - 1) for i in range(1, 4)])


def gelu_parts(values):
    cumulative = 0.5 * (1.0 + lax.erf(values * half_root))
    density = jnp.exp(-0.5 * values * values) * density_factor
    return (values * cumulative, cumulative + values * density)


def dot_trans(left, right):
    return lax.dot_general(
        left, right, (((1,), (1,)), ((), ())), preferred_element_type=jnp.float32
    )


def trans_dot(left, right):
    return lax.dot_general(
        left, right, (((0,), (0,)), ((), ())), preferred_element_type=jnp.float32
    )


def whole(shape):
    return pl.BlockSpec(shape, lambda n, *_: (0,) * len(shape))


def columns(rows, width):
    return pl.BlockSpec((rows, width), lambda n, *_: (0, n))


def hidden_kernel(rows, places, *refs):
    pieces, weight = refs[:8], refs[8]
    ordered, to_right, to_left, right_top, left_bottom, own = refs[9:]

    @pl.when(pl.program_id(0) == 0)
    def _():
        for place, piece in enumerate(pieces):
            start = pl.multiple_of(places[place], rows)
            ordered[pl.ds(start, rows), :] = piece[...]

    product = dot_trans(ordered[...], weight[...])
    own[...] = product[: 2 * rows]
    right_top[...] = product[2 * rows : 3 * rows]
    to_right[rows:, :] = product[3 * rows : 4 * rows]
    to_right[:rows, :] = product[4 * rows : 5 * rows]
    to_left[rows:, :] = product[5 * rows : 6 * rows]
    to_left[:rows, :] = product[6 * rows : 7 * rows]
    left_bottom[...] = product[7 * rows :]


def hidden_parts(places, pieces, weight, tile=512):
    rows, depth = pieces[0].shape
    width = weight.shape[0]
    heights = (2 * rows, 2 * rows, rows, rows, 2 * rows)
    return pl.pallas_call(
        functools.partial(hidden_kernel, rows),
        grid_spec=pltpu.PrefetchScalarGridSpec(
            num_scalar_prefetch=1,
            grid=(width // tile,),
            in_specs=[whole((rows, depth))] * 8
            + [pl.BlockSpec((tile, depth), lambda n, *_: (n, 0))],
            out_specs=[whole((8 * rows, depth))] + [columns(h, tile) for h in heights],
        ),
        out_shape=[jax.ShapeDtypeStruct((8 * rows, depth), jnp.bfloat16)]
        + [jax.ShapeDtypeStruct((h, width), jnp.float32) for h in heights],
        compiler_params=pltpu.CompilerParams(vmem_limit_bytes=vmem_bytes),
        cost_estimate=pl.CostEstimate(
            flops=16 * rows * depth * width,
            bytes_accessed=2 * width * depth + 32 * rows * depth + 32 * rows * width,
            transcendentals=0,
        ),
    )(places, *pieces, weight)


def normed_kernel(rows, places, *refs):
    own, right, far_top, far_bottom, left, weight = refs[:6]
    ordered, mine, plane, far_plane, to_up, to_down, far, up_top, down_bottom = refs[6:15]
    held = refs[15]
    half = rows // 2

    @pl.when(pl.program_id(0) == 0)
    def _():
        held[: 2 * rows, :] = own[...]
        held[2 * rows : 4 * rows, :] = right[...]
        held[4 * rows : 5 * rows, :] = far_top[...]
        held[5 * rows : 6 * rows, :] = far_bottom[...]
        held[6 * rows :, :] = left[...]
        for place in range(8):
            start = pl.multiple_of(places[place], rows)
            ordered[place * rows : (place + 1) * rows, :] = held[pl.ds(start, rows), :]

    product = dot_trans(ordered[...], weight[...])
    block = lambda place: product[place * rows : (place + 1) * rows]
    mine[...] = block(0)
    up_top[...] = block(1)[:half]
    to_up[rows:, :] = block(1)[half:]
    far[...] = block(2)
    to_down[rows:, :] = block(3)[:half]
    down_bottom[...] = block(3)[half:]
    plane[...] = block(4)
    to_up[:rows, :] = block(5)
    far_plane[...] = block(6)
    to_down[:rows, :] = block(7)


def normed_parts(places, pieces, weight, tile=512):
    rows, depth = pieces[2].shape
    width = weight.shape[0]
    half = rows // 2
    heights = (rows, rows, rows, rows + half, rows + half, rows, half, half)
    return pl.pallas_call(
        functools.partial(normed_kernel, rows),
        grid_spec=pltpu.PrefetchScalarGridSpec(
            num_scalar_prefetch=1,
            grid=(width // tile,),
            in_specs=[whole(piece.shape) for piece in pieces]
            + [pl.BlockSpec((tile, depth), lambda n, *_: (n, 0))],
            out_specs=[whole((8 * rows, depth))] + [columns(h, tile) for h in heights],
            scratch_shapes=[pltpu.VMEM((8 * rows, depth), jnp.bfloat16)],
        ),
        out_shape=[jax.ShapeDtypeStruct((8 * rows, depth), jnp.bfloat16)]
        + [jax.ShapeDtypeStruct((h, width), jnp.float32) for h in heights],
        compiler_params=pltpu.CompilerParams(vmem_limit_bytes=vmem_bytes),
        cost_estimate=pl.CostEstimate(
            flops=16 * rows * depth * width,
            bytes_accessed=2 * width * depth + 32 * rows * depth + 32 * rows * width,
            transcendentals=0,
        ),
    )(places, *pieces, weight)


def weight_kernel(cuts, sizes, *refs):
    count = len(cuts)
    pieces = refs[: len(refs) - count - 2]
    chunks, result, held = refs[len(pieces) : len(pieces) + count], refs[-2], refs[-1]
    total = None
    for chunk, cut in zip(chunks, cuts):
        at = 0
        for piece, first, rows in cut:
            held[at : at + rows, :] = pieces[piece][first : first + rows, :]
            at += rows
        term = trans_dot(held[:at, :], chunk[...])
        total = term if total is None else total + term
    result[0] = total.astype(result.dtype)


def weight_grad(pieces, cuts, chunks, tile=256):
    height = pieces[0].shape[1]
    width = chunks[0].shape[1]
    sizes = [chunk.shape[0] for chunk in chunks]
    return pl.pallas_call(
        functools.partial(weight_kernel, cuts, sizes),
        grid=(height // tile,),
        in_specs=[columns(piece.shape[0], tile) for piece in pieces]
        + [whole(chunk.shape) for chunk in chunks],
        out_specs=pl.BlockSpec((1, tile, width), lambda n: (0, n, 0)),
        out_shape=jax.ShapeDtypeStruct((1, height, width), jnp.bfloat16),
        scratch_shapes=[pltpu.VMEM((max(sizes), tile), jnp.bfloat16)],
        compiler_params=pltpu.CompilerParams(vmem_limit_bytes=vmem_bytes),
        cost_estimate=pl.CostEstimate(
            flops=2 * sum(sizes) * height * width,
            bytes_accessed=2 * (sum(sizes) * (height + width) + height * width),
            transcendentals=0,
        ),
    )(*pieces, *chunks)


def gather_col(block):
    beside = along_y(block)
    from_up, from_down = along_z(block, -1), along_z(block, 1)
    far = along_z(block, 2)
    beside_up, beside_down = along_z(beside, -1), along_z(beside, 1)
    beside_far = along_y(far)
    return [block, from_up, far, from_down, beside, beside_up, beside_far, beside_down]


def gather_row(block):
    half = block.shape[0] // 2
    from_right, from_left = along_x(block, -1), along_x(block, 1)
    far_top = along_x(from_left[:half], 1)
    far_bottom = along_x(from_right[half:], -1)
    return [block, from_right, far_top, far_bottom, from_left]


def sum_row(block):
    return (block + along_x(block, 2)) + (along_x(block, 1) + along_x(block, -1))


def sum_col(block):
    block = (block + along_z(block, 2)) + (along_z(block, 1) + along_z(block, -1))
    return block + along_y(block)


def local(inputs, cotangent, stashed, weight_in, weight_out, norm_gain):
    local_input = inputs[0]
    upstream = cotangent[0]
    hidden_pre = stashed[0]
    first_weight = weight_in[0]
    second_weight = weight_out[0]
    gains = norm_gain[0]
    width = gains.shape[0]
    feature_count = width * lax.axis_size("row")
    tokens = upstream.shape[0]
    row, col = lax.axis_index("row"), lax.axis_index("col")
    step = jnp.arange(8, dtype=jnp.int32)
    owner = (col // 4 + step // 4) % 2 * 4 + (col + step) % 4
    order = (owner // 2 - row + 4) % 4 * 2 + owner % 2

    starts, start = [], 0
    for rows in chunk_rows:
        starts.append(start)
        start += rows
    spans = list(zip(starts, chunk_rows))

    cot_pieces = [gather_col(upstream[s : s + r]) for s, r in spans]

    values = local_input.astype(jnp.float32)
    sums = jnp.stack([jnp.sum(values, axis=1), jnp.sum(values * values, axis=1)])
    sums = sum_row(sums)
    average = sums[0] / feature_count
    inv_scale = lax.rsqrt(sums[1] / feature_count - average * average + epsilon)
    standard = (values - average[:, None]) * inv_scale[:, None]
    normed_pieces = gather_col((standard * gains).astype(jnp.bfloat16))

    activated, slopes = gelu_parts(hidden_pre.astype(jnp.float32))
    activ_pieces = gather_row(activated.astype(jnp.bfloat16))

    cot_chunks, delta_chunks, received = [], [], []
    gain_part = None
    for (s, r), pieces in zip(spans, cot_pieces):
        places = order * r
        ordered, to_right, to_left, right_top, left_bottom, own = hidden_parts(
            places, pieces, second_weight
        )
        cot_chunks.append(ordered)
        from_left, from_right = along_x(to_right, 1), along_x(to_left, -1)
        top = along_x(right_top + from_left[:r], 1)
        bottom = along_x(left_bottom + from_right[r:], -1)
        top_slopes = slopes[s : s + r]
        bottom_slopes = slopes[tokens + s : tokens + s + r]
        deltas = jnp.concatenate(
            [
                ((own[:r] + from_right[:r]) + top) * top_slopes,
                ((own[r:] + from_left[r:]) + bottom) * bottom_slopes,
            ]
        ).astype(jnp.bfloat16)
        delta_pieces = gather_row(deltas)
        ordered, mine, plane, far_plane, to_up, to_down, far, up_top, down_bottom = (
            normed_parts(places, delta_pieces, first_weight)
        )
        delta_chunks.append(ordered)
        half = r // 2
        far = far + along_y(far_plane)
        from_down, from_up = along_z(to_up, 1), along_z(to_down, -1)
        plane = (plane + from_down[:r]) + from_up[:r]
        beside = along_y(plane)
        far_top, far_bottom = along_z(far[:half], 1), along_z(far[half:], -1)
        top = along_z(up_top + far_top, 1)
        bottom = along_z(down_bottom + far_bottom, -1)
        normed_grad = (mine + beside) + jnp.concatenate(
            [from_up[r:] + top, from_down[r:] + bottom]
        )
        chunk_standard = standard[s : s + r]
        part = jnp.sum(normed_grad * chunk_standard, axis=0)
        gain_part = part if gain_part is None else gain_part + part
        scaled_grad = normed_grad * gains
        means = sum_row(
            jnp.stack(
                [jnp.sum(scaled_grad, axis=1), jnp.sum(scaled_grad * chunk_standard, axis=1)]
            )
        )
        means = means / feature_count
        result_grad = upstream[s : s + r].astype(jnp.float32) + inv_scale[s : s + r, None] * (
            scaled_grad - means[0][:, None] - chunk_standard * means[1][:, None]
        )
        received.append(to_layer_before(result_grad.astype(jnp.bfloat16)))

    gain_grad = sum_col(gain_part[None])

    activ_cuts, normed_cuts = [], []
    for s, r in spans:
        activ_cuts.append(
            [
                (0, s, r),
                (0, tokens + s, r),
                (1, s, r),
                (1, tokens + s, r),
                (2, s, r),
                (3, s, r),
                (4, s, r),
                (4, tokens + s, r),
            ]
        )
        normed_cuts.append([(piece, s, r) for piece in range(8)])
    out_grad = weight_grad(activ_pieces, activ_cuts, cot_chunks)
    in_grad = weight_grad(normed_pieces, normed_cuts, delta_chunks)
    return (in_grad, out_grad, gain_grad, jnp.concatenate(received)[None])


def solution(mesh):
    return jax.shard_map(
        local,
        mesh=mesh,
        in_specs=(
            P("section", "col", "row"),
            P("section", "col", "row"),
            P("section", "row", "col"),
            P("section", "row", "col"),
            P("section", "col", "row"),
            P("section", "row"),
        ),
        out_specs=(
            P("section", "row", "col"),
            P("section", "col", "row"),
            P("section", "row"),
            P("section", "col", "row"),
        ),
        check_vma=False,
    )
```

time: 422 us -> 267 us (0.63)
  waiting for transfers between devices: 319 us -> 115 us
  starting transfers between devices: 5.39 us -> 97.3 us
  matrix products: 37.9 us -> 0 us
  blocking collectives: 36.7 us -> 0 us
  Pallas kernels: 0 us -> 32.5 us
  between operations: 14.1 us -> 1.31 us
  local copies, waits for them, and re-layouts: 1.08 us -> 9.24 us
    all_gather x4 -> x0, waiting for transfers between devices: 165 us -> none  [the longest x1 68 us: local(): grad_full = lax.all_gather(upstream, 'col', axis=0, tiled=True)]
    reduce_scatter x2 -> x0, waiting for transfers between devices: 152 us -> none  [the longest x1 90.3 us: local(): lax.psum_scatter(times_trans(delta_full, first_weight), 'col', scatter_di...]
    ppermute x1 -> x72, waiting for transfers between devices: 0.01 us -> 115 us  [the longest x29 68.3 us: along_x(): return lax.ppermute(block, 'row', [(i, (i + step) % 4) for i in range(4)])]
    ppermute x1 -> x72, starting transfers between devices: 5.15 us -> 97.3 us  [the longest x29 31 us: along_x(): return lax.ppermute(block, 'row', [(i, (i + step) % 4) for i in range(4)])]
    dot_general x4 -> x0, matrix products: 37.9 us -> none  [the longest x2 19.6 us: times_trans(): lax.dot_general(left, right, (((1,), (1,)), ((), ())), preferred_element_...]
    psum x3 -> x0, blocking collectives: 36.7 us -> none  [the longest x1 21.7 us: local(): gain_grad = lax.psum(jnp.sum(normed_grad * standard, axis=0), 'col')]
    pallas_call x0 -> x6, Pallas kernels: none -> 32.5 us  [the longest x2 14.6 us: weight_grad(): pl.pallas_call(functools.partial(weight_kernel, cuts, sizes), grid=(heigh...]
    unnamed x9 -> x36, local copies, waits for them, and re-layouts: 1.07 us -> 7.93 us
  transfers between devices with their start and end apart: 7 -> 72, of which waited for: 6 -> 24; matrix products, arithmetic and copies ran while one was open for 3% -> 4% of each run, Pallas kernels for 0% -> 12%
where the time goes in v1:
time: 267 us; the launch traced here: 266 us
  waiting for transfers between devices  115 us (43%)
  starting transfers between devices  97.3 us (36%)
  Pallas kernels  32.5 us (12%)
  other arithmetic  11.3 us (4%)
  local copies, waits for them, and re-layouts  9.24 us (3%)
    ppermute x29, waiting for transfers between devices, along_x(): return lax.ppermute(block, 'row', [(i, (i + step) % 4) for i in range(4)])  68.3 us
    ppermute x30, waiting for transfers between devices, along_z(): return lax.ppermute(block, 'col', route)  41.1 us
    ppermute x29, starting transfers between devices, along_x(): return lax.ppermute(block, 'row', [(i, (i + step) % 4) for i in range(4)])  31 us
    ppermute x30, starting transfers between devices, along_z(): return lax.ppermute(block, 'col', route)  30.5 us
    ppermute x2, starting transfers between devices, to_layer_before(): return lax.ppermute(block, 'section', [(i, i - 1) for i in range(1, 4)])  18.6 us
    ppermute x11, starting transfers between devices, along_y(): return lax.ppermute(block, 'col', [(j, (j + 4) % 8) for j in range(8)])  17.2 us
    pallas_call x2, Pallas kernels, weight_grad(): pl.pallas_call(functools.partial(weight_kernel, cuts, sizes), grid=(heigh...  14.6 us
    pallas_call x2, Pallas kernels, hidden_parts(): pl.pallas_call(functools.partial(hidden_kernel, rows), grid_spec=pltpu.Pr...  9.59 us
  transfers between devices with their start and end apart: 72, of which 24 were waited for; matrix products, arithmetic and copies ran while one was open for 4% of the time, Pallas kernels for 12%

profile of v1, /device:TPU:1, one launch (start us, length us, event | category | flops | bytes accessed | tf_op | source)
XLA Modules:
  0.0 266.4 jit_solution(10918687471130631767)
XLA Ops:
  1.7 3.8 %collective-permute-start.13 = (bf16[64,1536]{1,0:T(8,128)(2,1)S(1)}, bf16[64,1536]{1,0:T(8,128)(2,1)S(1)}, u32[]{:S(2)}, u32[]{:S(2)}) collective-permute-start(bf16[64,1536]{1,0:T(8,128)(2,1)S(1)} %get-tuple-element.91.refs_0_), channel_id=1, source_target_pairs={{0,4},{1,5},{2,6},{3,7},{4,0},{5,1},{6,2},{7,3},{8,12},{9,13},{10,... | collective-permute-start | bytes 589832 | tf_op jit(solution)/shard_map/ppermute | solution.py:28
  5.5 3.6 %collective-permute-start.11 = (bf16[64,1536]{1,0:T(8,128)(2,1)S(1)}, bf16[64,1536]{1,0:T(8,128)(2,1)S(1)}, u32[]{:S(2)}, u32[]{:S(2)}) collective-permute-start(bf16[64,1536]{1,0:T(8,128)(2,1)S(1)} %get-tuple-element.91.refs_0_), channel_id=1, source_target_pairs={{0,2},{1,3},{2,0},{3,1},{4,6},{5,7},{6,4},{7,5},{8,10},{9,11},{10,... | collective-permute-start | bytes 589832 | tf_op jit(solution)/shard_map/ppermute | solution.py:24
  31.3 4.5 %shard_map.93 = (bf16[512,1536]{1,0:T(8,128)(2,1)S(1)}, f32[128,1536]{1,0:T(8,128)}, f32[128,1536]{1,0:T(8,128)S(1)}, f32[64,1536]{1,0:T(8,128)S(1)}, f32[64,1536]{1,0:T(8,128)S(1)}, /*index=5*/f32[128,1536]{1,0:T(8,128)S(1)}) custom-call(s32[8]{0:T(128)S(1)} %fusion.29.places, bf16[64,1536]{1,0:T(8,128)(2,1)S(1)} %get-tuple-element.91.refs_0_, ...), custom_call_target="tpu_custom_call" | custom-call | flops 2415919104 | bytes 11010048 | tf_op jit(solution)/shard_map/pallas_call | solution.py:85
  36.9 3.4 %collective-permute-start.25 = (bf16[64,1536]{1,0:T(8,128)(2,1)S(1)}, bf16[64,1536]{1,0:T(8,128)(2,1)}, u32[]{:S(2)}, u32[]{:S(2)}) collective-permute-start(bf16[64,1536]{1,0:T(8,128)(2,1)S(1)} %get-tuple-element.90.refs_0_), channel_id=1, source_target_pairs={{0,3},{1,0},{2,1},{3,2},{4,7},{5,4},{6,5},{7,6},{8,11},{9,8},{10,9... | collective-permute-start | bytes 589832 | tf_op jit(solution)/shard_map/ppermute | solution.py:24
  54.9 5.1 %shard_map.95 = (bf16[512,1536]{1,0:T(8,128)(2,1)S(1)}, f32[128,1536]{1,0:T(8,128)S(1)}, f32[128,1536]{1,0:T(8,128)S(1)}, f32[64,1536]{1,0:T(8,128)S(1)}, f32[64...) custom-call(s32[8]{0:T(128)S(1)} %fusion.29.places, bf16[64,1536]{1,0:T(8,128)(2,1)S(1)} %get-tuple-element.90.refs_0_, ...), custom_call_target="tpu_custom_call" | custom-call | flops 2415919104 | bytes 11010048 | tf_op jit(solution)/shard_map/pallas_call | solution.py:85
  66.1 13.5 %collective-permute-done.32 = f32[128,1536]{1,0:T(8,128)S(1)} collective-permute-done((f32[128,1536]{1,0:T(8,128)S(1)}, f32[128,1536]{1,0:T(8,128)S(1)}, u32[]{:S(2)}, u32[]{:S(2)}) %collective-permute-start.32) | collective-permute-done | bytes 786464 | tf_op jit(solution)/shard_map/ppermute | solution.py:19
  79.7 3.4 %collective-permute-start.35 = (f32[64,1536]{1,0:T(8,128)S(1)}, f32[64,1536]{1,0:T(8,128)S(1)}, u32[]{:S(2)}, u32[]{:S(2)}) collective-permute-start(f32[64,1536]{1,0:T(8,128)S(1)} %slice_add_fusion.4), channel_id=1, source_target_pairs={{0,24},{8,0},{16,8},{24,16},{1,25},{9,1},{17,9},{25,17},{2,26},{10... | collective-permute-start | bytes 1179656 | tf_op jit(solution)/shard_map/ppermute | solution.py:19
  83.1 9.8 %collective-permute-done.33 = f32[128,1536]{1,0:T(8,128)S(1)} collective-permute-done((f32[128,1536]{1,0:T(8,128)S(1)}, f32[128,1536]{1,0:T(8,128)S(1)}, u32[]{:S(2)}, u32[]{:S(2)}) %collective-permute-start.33) | collective-permute-done | bytes 786464 | tf_op jit(solution)/shard_map/ppermute | solution.py:19
  93.3 8.1 %collective-permute-done.19 = f32[64,1536]{1,0:T(8,128)S(1)} collective-permute-done((f32[64,1536]{1,0:T(8,128)S(1)}, f32[64,1536]{1,0:T(8,128)S(1)}, u32[]{:S(2)}, u32[]{:S(2)}) %collective-permute-start.19) | collective-permute-done | bytes 393248 | tf_op jit(solution)/shard_map/ppermute | solution.py:19
  101.4 8.4 %collective-permute-done.34 = f32[64,1536]{1,0:T(8,128)S(1)} collective-permute-done((f32[64,1536]{1,0:T(8,128)S(1)}, f32[64,1536]{1,0:T(8,128)S(1)}, u32[]{:S(2)}, u32[]{:S(2)}) %collective-permute-start.34) | collective-permute-done | bytes 393248 | tf_op jit(solution)/shard_map/ppermute | solution.py:19
  117.5 3.3 %collective-permute-done.22.refs_4_ = bf16[128,1536]{1,0:T(8,128)(2,1)S(1)} collective-permute-done((bf16[128,1536]{1,0:T(8,128)(2,1)S(1)}, bf16[128,1536]{1,0:T(8,128)(2,1)S(1)}, u32[]{:S(2)}, u32[]{:S(2)}) %collective-permute-start.22) | collective-permute-done | bytes 393248 | tf_op jit(solution)/shard_map/ppermute | solution.py:19
  124.2 5.1 %collective-permute-done.37.refs_4_ = bf16[128,1536]{1,0:T(8,128)(2,1)S(1)} collective-permute-done((bf16[128,1536]{1,0:T(8,128)(2,1)S(1)}, bf16[128,1536]{1,0:T(8,128)(2,1)S(1)}, u32[]{:S(2)}, u32[]{:S(2)}) %collective-permute-start.37) | collective-permute-done | bytes 393248 | tf_op jit(solution)/shard_map/ppermute | solution.py:19
  132.6 9.3 %collective-permute-done.23.refs_2_ = bf16[64,1536]{1,0:T(8,128)(2,1)S(1)} collective-permute-done((bf16[64,1536]{1,0:T(8,128)(2,1)S(1)}, bf16[64,1536]{1,0:T(8,128)(2,1)S(1)}, u32[]{:S(2)}, u32[]{:S(2)}) %collective-permute-start.23) | collective-permute-done | bytes 196640 | tf_op jit(solution)/shard_map/ppermute | solution.py:19
  141.9 3.3 %collective-permute-done.24.refs_3_ = bf16[64,1536]{1,0:T(8,128)(2,1)S(1)} collective-permute-done((bf16[64,1536]{1,0:T(8,128)(2,1)S(1)}, bf16[64,1536]{1,0:T(8,128)(2,1)S(1)}, u32[]{:S(2)}, u32[]{:S(2)}) %collective-permute-start.24) | collective-permute-done | bytes 196640 | tf_op jit(solution)/shard_map/ppermute | solution.py:19
  145.2 4.1 %shard_map.94 = (bf16[512,1536]{1,0:T(8,128)(2,1)S(1)}, f32[64,1536]{1,0:T(8,128)S(1)}, f32[64,1536]{1,0:T(8,128)S(1)}, f32[64,1536]{1,0:T(8,128)S(1)}, f32[96,1...) custom-call(s32[8]{0:T(128)S(1)} %fusion.29.places, ...), custom_call_target="tpu_custom_call" | custom-call | flops 2415919104 | bytes 11010048 | tf_op jit(solution)/shard_map/pallas_call | solution.py:141
  149.5 7.3 %shard_map.98 = bf16[1,1536,1536]{2,1,0:T(8,128)(2,1)} custom-call(bf16[256,1536]{1,0:T(8,128)(2,1)S(1)} %get-tuple-element.82.refs_0_, bf16[256,1536]{1,0:T(8,128)(2,1)S(1)} %collective-permute-done.40.refs_1_, bf16[128,1536]{1,0:T(8,128)(2,1)S(1)} %collective-permute-done.42.refs_2_, bf16[128,1536]{1,0:T(8,128)(2,1)S(1)} %collective-permute-done.43.refs_3_, ...), custom_call_target="tpu_custom_call" | custom-call | flops 4831838208 | bytes 11010048 | tf_op jit(solution)/shard_map/pallas_call | solution.py:181
  159.4 4.1 %shard_map.96 = (bf16[512,1536]{1,0:T(8,128)(2,1)S(1)}, f32[64,1536]{1,0:T(8,128)S(1)}, f32[64,1536]{1,0:T(8,128)S(1)}, f32[64,1536]{1,0:T(8,128)S(1)}, f32[96,1...) custom-call(s32[8]{0:T(128)S(1)} %fusion.29.places, ...), custom_call_target="tpu_custom_call" | custom-call | flops 2415919104 | bytes 11010048 | tf_op jit(solution)/shard_map/pallas_call | solution.py:141
  169.3 5.1 %collective-permute-done.55 = f32[64,1536]{1,0:T(8,128)S(1)} collective-permute-done((f32[64,1536]{1,0:T(8,128)S(1)}, f32[64,1536]{1,0:T(8,128)S(1)}, u32[]{:S(2)}, u32[]{:S(2)}) %collective-permute-start.55) | collective-permute-done | bytes 393248 | tf_op jit(solution)/shard_map/ppermute | solution.py:28
  174.5 8.5 %collective-permute-done.48 = f32[32,1536]{1,0:T(8,128)S(1)} collective-permute-done((f32[32,1536]{1,0:T(8,128)S(1)}, f32[32,1536]{1,0:T(8,128)S(1)}, u32[]{:S(2)}, u32[]{:S(2)}) %collective-permute-start.48) | collective-permute-done | bytes 196640 | tf_op jit(solution)/shard_map/ppermute | solution.py:24
  194.6 4.4 %collective-permute-done.49 = f32[32,1536]{1,0:T(8,128)S(1)} collective-permute-done((f32[32,1536]{1,0:T(8,128)S(1)}, f32[32,1536]{1,0:T(8,128)S(1)}, u32[]{:S(2)}, u32[]{:S(2)}) %collective-permute-start.49) | collective-permute-done | bytes 196640 | tf_op jit(solution)/shard_map/ppermute | solution.py:24
  201.9 11.7 %collective-permute-done.57 = f32[32,1536]{1,0:T(8,128)S(1)} collective-permute-done((f32[32,1536]{1,0:T(8,128)S(1)}, f32[32,1536]{1,0:T(8,128)S(1)}, u32[]{:S(2)}, u32[]{:S(2)}) %collective-permute-start.57) | collective-permute-done | bytes 196640 | tf_op jit(solution)/shard_map/ppermute | solution.py:24
  213.7 4.5 %collective-permute-done.59 = f32[32,1536]{1,0:T(8,128)S(1)} collective-permute-done((f32[32,1536]{1,0:T(8,128)S(1)}, f32[32,1536]{1,0:T(8,128)S(1)}, u32[]{:S(2)}, u32[]{:S(2)}) %collective-permute-start.59) | collective-permute-done | bytes 196640 | tf_op jit(solution)/shard_map/ppermute | solution.py:24
  238.6 16.7 %collective-permute-start.67 = (bf16[64,1536]{1,0:T(8,128)(2,1)S(1)}, bf16[64,1536]{1,0:T(8,128)(2,1)S(1)}, u32[]{:S(2)}, u32[]{:S(2)}) collective-permute-start(bf16[64,1536]{1,0:T(8,128)(2,1)S(1)} %get-tuple-element.80), channel_id=1, source_target_pairs={{32,0},{64,32},{96,64},{33,1},{65,33},{97,65},{34,2},{66,34},{98,6... | collective-permute-start | bytes 589832 | tf_op jit(solution)/shard_map/ppermute | solution.py:32
  257.6 7.4 %shard_map.97 = bf16[1,1536,1536]{2,1,0:T(8,128)(2,1)} custom-call(bf16[128,1536]{1,0:T(8,128)(2,1)S(1)} %get-tuple-element.85.refs_0_, bf16[128,1536]{1,0:T(8,128)(2,1)S(1)} %collective-permute-done.3.refs_1_, bf16[128,1536]{1,0:T(8,128)(2,1)S(1)} %collective-permute-done.4.refs_2_, bf16[128,1536]{1,0:T(8,128)(2,1)S(1)} %collective-permute-done.5.refs_3_, ...), custom_call_target="tpu_custom_call" | custom-call | flops 4831838208 | bytes 11010048 | tf_op jit(solution)/shard_map/pallas_call | solution.py:181
  (215 shorter events, 106.5 us)
Async XLA Ops:
  18.4 25.1 %collective-permute-start.28 = (bf16[64,1536]{1,0:T(8,128)(2,1)S(1)}, bf16[64,1536]{1,0:T(8,128)(2,1)S(1)}, u32[]{:S(2)}, u32[]{:S(2)}) collective-permute-start(bf16[64,1536]{1,0:T(8,128)(2,1)S(1)} %get-tuple-element.90.refs_0_), channel_id=1, source_target_pairs={{0,4},{1,5},{2,6},{3,7},{4,0},{5,1},{6,2},{7,3},{8,12},{9,13},{10,... | collective-permute-start | bytes 589832 | tf_op jit(solution)/shard_map/ppermute | solution.py:28
  19.1 27.1 %collective-permute-start.26 = (bf16[64,1536]{1,0:T(8,128)(2,1)S(1)}, bf16[64,1536]{1,0:T(8,128)(2,1)}, u32[]{:S(2)}, u32[]{:S(2)}) collective-permute-start(bf16[64,1536]{1,0:T(8,128)(2,1)S(1)} %get-tuple-element.90.refs_0_), channel_id=1, source_target_pairs={{0,2},{1,3},{2,0},{3,1},{4,6},{5,7},{6,4},{7,5},{8,10},{9,11},{10,... | collective-permute-start | bytes 589832 | tf_op jit(solution)/shard_map/ppermute | solution.py:24
  40.4 21.8 %collective-permute-start.18 = (f32[128,1536]{1,0:T(8,128)}, f32[128,1536]{1,0:T(8,128)}, u32[]{:S(2)}, u32[]{:S(2)}) collective-permute-start(f32[128,1536]{1,0:T(8,128)} %get-tuple-element.37), channel_id=1, source_target_pairs={{0,8},{8,16},{16,24},{24,0},{1,9},{9,17},{17,25},{25,1},{2,10},{10... | collective-permute-start | bytes 2359304 | tf_op jit(solution)/shard_map/ppermute | solution.py:19
  49.3 65.1 %collective-permute-start.41 = (bf16[256,1536]{1,0:T(8,128)(2,1)S(1)}, bf16[256,1536]{1,0:T(8,128)(2,1)S(1)}, u32[]{:S(2)}, u32[]{:S(2)}) collective-permute-start(bf16[256,1536]{1,0:T(8,128)(2,1)S(1)} %get-tuple-element.82.refs_0_), channel_id=1, source_target_pairs={{0,8},{8,16},{16,24},{24,0},{1,9},{9,17},{17,25},{25,1},{2,10},{10... | collective-permute-start | bytes 2359304 | tf_op jit(solution)/shard_map/ppermute | solution.py:19
  60.0 19.7 %collective-permute-start.32 = (f32[128,1536]{1,0:T(8,128)S(1)}, f32[128,1536]{1,0:T(8,128)S(1)}, u32[]{:S(2)}, u32[]{:S(2)}) collective-permute-start(f32[128,1536]{1,0:T(8,128)S(1)} %get-tuple-element.41), channel_id=1, source_target_pairs={{0,24},{8,0},{16,8},{24,16},{1,25},{9,1},{17,9},{25,17},{2,26},{10... | collective-permute-start | bytes 2359304 | tf_op jit(solution)/shard_map/ppermute | solution.py:19
  62.2 30.8 %collective-permute-start.33 = (f32[128,1536]{1,0:T(8,128)S(1)}, f32[128,1536]{1,0:T(8,128)S(1)}, u32[]{:S(2)}, u32[]{:S(2)}) collective-permute-start(f32[128,1536]{1,0:T(8,128)S(1)} %get-tuple-element.43), channel_id=1, source_target_pairs={{0,8},{8,16},{16,24},{24,0},{1,9},{9,17},{17,25},{25,1},{2,10},{10... | collective-permute-start | bytes 2359304 | tf_op jit(solution)/shard_map/ppermute | solution.py:19
  63.2 38.2 %collective-permute-start.19 = (f32[64,1536]{1,0:T(8,128)S(1)}, f32[64,1536]{1,0:T(8,128)S(1)}, u32[]{:S(2)}, u32[]{:S(2)}) collective-permute-start(f32[64,1536]{1,0:T(8,128)S(1)} %slice_add_fusion.10), channel_id=1, source_target_pairs={{0,8},{8,16},{16,24},{24,0},{1,9},{9,17},{17,25},{25,1},{2,10},{10... | collective-permute-start | bytes 1179656 | tf_op jit(solution)/shard_map/ppermute | solution.py:19
  63.4 38.0 %collective-permute-start.20 = (f32[64,1536]{1,0:T(8,128)S(1)}, f32[64,1536]{1,0:T(8,128)S(1)}, u32[]{:S(2)}, u32[]{:S(2)}) collective-permute-start(f32[64,1536]{1,0:T(8,128)S(1)} %slice_add_fusion.8), channel_id=1, source_target_pairs={{0,24},{8,0},{16,8},{24,16},{1,25},{9,1},{17,9},{25,17},{2,26},{10... | collective-permute-start | bytes 1179656 | tf_op jit(solution)/shard_map/ppermute | solution.py:19
  79.7 21.7 %collective-permute-start.35 = (f32[64,1536]{1,0:T(8,128)S(1)}, f32[64,1536]{1,0:T(8,128)S(1)}, u32[]{:S(2)}, u32[]{:S(2)}) collective-permute-start(f32[64,1536]{1,0:T(8,128)S(1)} %slice_add_fusion.4), channel_id=1, source_target_pairs={{0,24},{8,0},{16,8},{24,16},{1,25},{9,1},{17,9},{25,17},{2,26},{10... | collective-permute-start | bytes 1179656 | tf_op jit(solution)/shard_map/ppermute | solution.py:19
  117.4 32.1 %collective-permute-start.42 = (bf16[128,1536]{1,0:T(8,128)(2,1)S(1)}, bf16[128,1536]{1,0:T(8,128)(2,1)S(1)}, u32[]{:S(2)}, u32[]{:S(2)}) collective-permute-start(bf16[128,1536]{1,0:T(8,128)(2,1)S(1)} %slice.210), channel_id=1, source_target_pairs={{0,8},{8,16},{16,24},{24,0},{1,9},{9,17},{17,25},{25,1},{2,10},{10... | collective-permute-start | bytes 1179656 | tf_op jit(solution)/shard_map/ppermute | solution.py:19
  120.8 28.6 %collective-permute-start.43 = (bf16[128,1536]{1,0:T(8,128)(2,1)S(1)}, bf16[128,1536]{1,0:T(8,128)(2,1)S(1)}, u32[]{:S(2)}, u32[]{:S(2)}) collective-permute-start(bf16[128,1536]{1,0:T(8,128)(2,1)S(1)} %slice.211), channel_id=1, source_target_pairs={{0,24},{8,0},{16,8},{24,16},{1,25},{9,1},{17,9},{25,17},{2,26},{10... | collective-permute-start | bytes 1179656 | tf_op jit(solution)/shard_map/ppermute | solution.py:19
  132.6 26.9 %collective-permute-start.38 = (bf16[64,1536]{1,0:T(8,128)(2,1)S(1)}, bf16[64,1536]{1,0:T(8,128)(2,1)S(1)}, u32[]{:S(2)}, u32[]{:S(2)}) collective-permute-start(bf16[64,1536]{1,0:T(8,128)(2,1)S(1)} %slice.208), channel_id=1, source_target_pairs={{0,8},{8,16},{16,24},{24,0},{1,9},{9,17},{17,25},{25,1},{2,10},{10... | collective-permute-start | bytes 589832 | tf_op jit(solution)/shard_map/ppermute | solution.py:19
  156.7 29.1 %collective-permute-start.44 = (f32[96,1536]{1,0:T(8,128)S(1)}, f32[96,1536]{1,0:T(8,128)S(1)}, u32[]{:S(2)}, u32[]{:S(2)}) collective-permute-start(f32[96,1536]{1,0:T(8,128)S(1)} %get-tuple-element.50), channel_id=1, source_target_pairs={{0,1},{1,2},{2,3},{3,0},{4,5},{5,6},{6,7},{7,4},{8,9},{9,10},{10,1... | collective-permute-start | bytes 1769480 | tf_op jit(solution)/shard_map/ppermute | solution.py:24
  156.7 29.2 %collective-permute-start.45 = (f32[96,1536]{1,0:T(8,128)S(1)}, f32[96,1536]{1,0:T(8,128)S(1)}, u32[]{:S(2)}, u32[]{:S(2)}) collective-permute-start(f32[96,1536]{1,0:T(8,128)S(1)} %get-tuple-element.51), channel_id=1, source_target_pairs={{0,3},{1,0},{2,1},{3,2},{4,7},{5,4},{6,5},{7,6},{8,11},{9,8},{10,9... | collective-permute-start | bytes 1769480 | tf_op jit(solution)/shard_map/ppermute | solution.py:24
  163.5 23.9 %collective-permute-start.52 = (f32[96,1536]{1,0:T(8,128)S(1)}, f32[96,1536]{1,0:T(8,128)S(1)}, u32[]{:S(2)}, u32[]{:S(2)}) collective-permute-start(f32[96,1536]{1,0:T(8,128)S(1)} %get-tuple-element.58), channel_id=1, source_target_pairs={{0,1},{1,2},{2,3},{3,0},{4,5},{5,6},{6,7},{7,4},{8,9},{9,10},{10,1... | collective-permute-start | bytes 1769480 | tf_op jit(solution)/shard_map/ppermute | solution.py:24
  163.6 25.2 %collective-permute-start.53 = (f32[96,1536]{1,0:T(8,128)S(1)}, f32[96,1536]{1,0:T(8,128)S(1)}, u32[]{:S(2)}, u32[]{:S(2)}) collective-permute-start(f32[96,1536]{1,0:T(8,128)S(1)} %get-tuple-element.59), channel_id=1, source_target_pairs={{0,3},{1,0},{2,1},{3,2},{4,7},{5,4},{6,5},{7,6},{8,11},{9,8},{10,9... | collective-permute-start | bytes 1769480 | tf_op jit(solution)/shard_map/ppermute | solution.py:24
  183.0 48.6 %collective-permute-start.6 = (bf16[128,1536]{1,0:T(8,128)(2,1)S(1)}, bf16[128,1536]{1,0:T(8,128)(2,1)S(1)}, u32[]{:S(2)}, u32[]{:S(2)}) collective-permute-start(bf16[128,1536]{1,0:T(8,128)(2,1)S(1)} %get-tuple-element.85.refs_0_), channel_id=1, source_target_pairs={{0,4},{1,5},{2,6},{3,7},{4,0},{5,1},{6,2},{7,3},{8,12},{9,13},{10,... | collective-permute-start | bytes 1179656 | tf_op jit(solution)/shard_map/ppermute | solution.py:28
  190.8 40.9 %collective-permute-start.4 = (bf16[128,1536]{1,0:T(8,128)(2,1)S(1)}, bf16[128,1536]{1,0:T(8,128)(2,1)S(1)}, u32[]{:S(2)}, u32[]{:S(2)}) collective-permute-start(bf16[128,1536]{1,0:T(8,128)(2,1)S(1)} %get-tuple-element.85.refs_0_), channel_id=1, source_target_pairs={{0,2},{1,3},{2,0},{3,1},{4,6},{5,7},{6,4},{7,5},{8,10},{9,11},{10,... | collective-permute-start | bytes 1179656 | tf_op jit(solution)/shard_map/ppermute | solution.py:24
  192.7 25.5 %collective-permute-start.46 = (f32[64,1536]{1,0:T(8,128)S(1)}, f32[64,1536]{1,0:T(8,128)S(1)}, u32[]{:S(2)}, u32[]{:S(2)}) collective-permute-start(f32[64,1536]{1,0:T(8,128)S(1)} %slice_add_fusion.2), channel_id=1, source_target_pairs={{0,4},{1,5},{2,6},{3,7},{4,0},{5,1},{6,2},{7,3},{8,12},{9,13},{10,... | collective-permute-start | bytes 1179656 | tf_op jit(solution)/shard_map/ppermute | solution.py:28
  231.7 23.6 %collective-permute-start.5 = (bf16[128,1536]{1,0:T(8,128)(2,1)S(1)}, bf16[128,1536]{1,0:T(8,128)(2,1)S(1)}, u32[]{:S(2)}, u32[]{:S(2)}) collective-permute-start(bf16[128,1536]{1,0:T(8,128)(2,1)S(1)} %get-tuple-element.85.refs_0_), channel_id=1, source_target_pairs={{0,1},{1,2},{2,3},{3,0},{4,5},{5,6},{6,7},{7,4},{8,9},{9,10},{10,1... | collective-permute-start | bytes 1179656 | tf_op jit(solution)/shard_map/ppermute | solution.py:24
  233.1 24.1 %collective-permute-start.7 = (bf16[128,1536]{1,0:T(8,128)(2,1)S(1)}, bf16[128,1536]{1,0:T(8,128)(2,1)S(1)}, u32[]{:S(2)}, u32[]{:S(2)}) collective-permute-start(bf16[128,1536]{1,0:T(8,128)(2,1)S(1)} %collective-permute-done.6.refs_4_), channel_id=1, source_target_pairs={{0,3},{1,0},{2,1},{3,2},{4,7},{5,4},{6,5},{7,6},{8,11},{9,8},{10,9... | collective-permute-start | bytes 1179656 | tf_op jit(solution)/shard_map/ppermute | solution.py:24
  234.5 23.2 %collective-permute-start.9 = (bf16[128,1536]{1,0:T(8,128)(2,1)S(1)}, bf16[128,1536]{1,0:T(8,128)(2,1)S(1)}, u32[]{:S(2)}, u32[]{:S(2)}) collective-permute-start(bf16[128,1536]{1,0:T(8,128)(2,1)S(1)} %collective-permute-done.6.refs_4_), channel_id=1, source_target_pairs={{0,1},{1,2},{2,3},{3,0},{4,5},{5,6},{6,7},{7,4},{8,9},{9,10},{10,1... | collective-permute-start | bytes 1179656 | tf_op jit(solution)/shard_map/ppermute | solution.py:24
  234.6 23.0 %collective-permute-start.8 = (bf16[128,1536]{1,0:T(8,128)(2,1)S(1)}, bf16[128,1536]{1,0:T(8,128)(2,1)S(1)}, u32[]{:S(2)}, u32[]{:S(2)}) collective-permute-start(bf16[128,1536]{1,0:T(8,128)(2,1)S(1)} %collective-permute-done.4.refs_2_), channel_id=1, source_target_pairs={{0,4},{1,5},{2,6},{3,7},{4,0},{5,1},{6,2},{7,3},{8,12},{9,13},{10,... | collective-permute-start | bytes 1179656 | tf_op jit(solution)/shard_map/ppermute | solution.py:28
  238.6 27.0 %collective-permute-start.67 = (bf16[64,1536]{1,0:T(8,128)(2,1)S(1)}, bf16[64,1536]{1,0:T(8,128)(2,1)S(1)}, u32[]{:S(2)}, u32[]{:S(2)}) collective-permute-start(bf16[64,1536]{1,0:T(8,128)(2,1)S(1)} %get-tuple-element.80), channel_id=1, source_target_pairs={{32,0},{64,32},{96,64},{33,1},{65,33},{97,65},{34,2},{66,34},{98,6... | collective-permute-start | bytes 589832 | tf_op jit(solution)/shard_map/ppermute | solution.py:32
  (66 other events, 693.2 us)

commit v2 on v0

v2 whole, which is shorter than its diff:
```python
import functools

import jax
import jax.numpy as jnp
from jax import lax
from jax.experimental import pallas as pl
from jax.experimental.pallas import tpu as pltpu
from jax.sharding import PartitionSpec as P

epsilon = 1e-06
half_root = 0.7071067811865476
density_factor = 0.3989422804014327

chunk_rows = (64, 64)
vmem_bytes = 60 * 1024 * 1024


def along_x(block, step):
    return lax.ppermute(block, "row", [(i, (i + step) % 4) for i in range(4)])


def along_z(block, step):
    route = [(j, j // 4 * 4 + (j % 4 + step) % 4) for j in range(8)]
    return lax.ppermute(block, "col", route)


def along_y(block):
    return lax.ppermute(block, "col", [(j, (j + 4) % 8) for j in range(8)])


def to_layer_before(block):
    return lax.ppermute(block, "section", [(i, i - 1) for i in range(1, 4)])


def gelu_parts(values):
    cumulative = 0.5 * (1.0 + lax.erf(values * half_root))
    density = jnp.exp(-0.5 * values * values) * density_factor
    return (values * cumulative, cumulative + values * density)


def dot_trans(left, right):
    return lax.dot_general(
        left, right, (((1,), (1,)), ((), ())), preferred_element_type=jnp.float32
    )


def trans_dot(left, right):
    return lax.dot_general(
        left, right, (((0,), (0,)), ((), ())), preferred_element_type=jnp.float32
    )


def whole(shape):
    return pl.BlockSpec(shape, lambda n, *_: (0,) * len(shape))


def columns(rows, width):
    return pl.BlockSpec((rows, width), lambda n, *_: (0, n))


def hidden_kernel(spans, tile, after, places, *refs):
    def source(pieces, block, rows):
        return pieces[block], 0

    def give(outputs, product, rows):
        own, to_right, to_left, right_top, left_bottom = outputs
        own[...] = product[: 2 * rows]
        right_top[...] = product[2 * rows : 3 * rows]
        to_right[rows:, :] = product[3 * rows : 4 * rows]
        to_right[:rows, :] = product[4 * rows : 5 * rows]
        to_left[rows:, :] = product[5 * rows : 6 * rows]
        to_left[:rows, :] = product[6 * rows : 7 * rows]
        left_bottom[...] = product[7 * rows :]

    tiled_products(spans, tile, 8, after, places, refs, source, give)


def normed_kernel(spans, tile, after, places, *refs):
    def source(pieces, block, rows):
        return pieces[block // 2], block % 2 * rows

    def give(outputs, product, rows):
        mine, to_up, to_down, up_same, down_other = outputs
        block = lambda place: product[place * rows : (place + 1) * rows]
        mine[:rows, :] = block(0)
        up_same[...] = block(1)
        to_up[:rows, :] = block(2)
        to_down[:rows, :] = block(3)
        mine[rows:, :] = block(4)
        to_up[rows:, :] = block(5)
        to_down[rows:, :] = block(6)
        down_other[...] = block(7)

    tiled_products(spans, tile, 4, after, places, refs, source, give)


def tiled_products(spans, tile, count, after, places, refs, source, give):
    chunks = len(spans)
    pieces, weight, refs = refs[:count], refs[count], refs[count + 1 + after :]
    kept, outputs = refs[:chunks], refs[chunks : 6 * chunks]
    held, arrived, fetched, saved = refs[6 * chunks :]
    step = pl.program_id(0)

    def weight_copy(index):
        place = pl.ds(index * tile, tile)
        return pltpu.make_async_copy(
            weight.at[place, :], held.at[place, :], fetched.at[index]
        )

    tiles = weight.shape[0] // tile
    bases, base = [], weight.shape[0]
    for _, rows in spans:
        bases.append(base)
        base += 8 * rows

    def save_copy(index):
        return pltpu.make_async_copy(
            held.at[pl.ds(bases[index], 8 * spans[index][1]), :], kept[index], saved.at[index]
        )

    @pl.when(step == 0)
    def _():
        copies = []
        for (first, rows), base in zip(spans, bases):
            for block in range(8):
                piece, offset = source(pieces, block, rows)
                start = pl.multiple_of(base + places[block] * rows, 16)
                copies.append(
                    pltpu.make_async_copy(
                        piece.at[pl.ds(first + offset, rows), :],
                        held.at[pl.ds(start, rows), :],
                        arrived.at[len(copies)],
                    )
                )
        for copy in copies:
            copy.start()
        for index in range(tiles):
            weight_copy(index).start()
        for copy in copies:
            copy.wait()
        for index in range(chunks):
            save_copy(index).start()

    for index in range(tiles):

        @pl.when(step == index)
        def _():
            weight_copy(index).wait()

    part = held[pl.ds(pl.multiple_of(step * tile, tile), tile), :]
    for index, (_, rows) in enumerate(spans):
        rhs = held[bases[index] : bases[index] + 8 * rows, :]
        give(outputs[5 * index : 5 * index + 5], dot_trans(rhs, part), rows)

    @pl.when(step == tiles - 1)
    def _():
        for index in range(chunks):
            save_copy(index).wait()


def parts_of(kernel, places, pieces, weight, spans, after=(), tile=256):
    width, depth = weight.shape
    rows = sum(8 * r for _, r in spans)
    chunks = len(spans)
    heights = [h for _, r in spans for h in (2 * r, 2 * r, 2 * r, r, r)]
    results = pl.pallas_call(
        functools.partial(kernel, spans, tile, len(after)),
        grid_spec=pltpu.PrefetchScalarGridSpec(
            num_scalar_prefetch=1,
            grid=(width // tile,),
            in_specs=[pl.BlockSpec(memory_space=pl.ANY)] * (len(pieces) + 1 + len(after)),
            out_specs=[pl.BlockSpec(memory_space=pl.ANY)] * chunks
            + [columns(h, tile) for h in heights],
            scratch_shapes=[
                pltpu.VMEM((width + rows, depth), jnp.bfloat16),
                pltpu.SemaphoreType.DMA((8 * chunks,)),
                pltpu.SemaphoreType.DMA((width // tile,)),
                pltpu.SemaphoreType.DMA((chunks,)),
            ],
        ),
        out_shape=[jax.ShapeDtypeStruct((8 * r, depth), jnp.bfloat16) for _, r in spans]
        + [jax.ShapeDtypeStruct((h, width), jnp.float32) for h in heights],
        compiler_params=pltpu.CompilerParams(vmem_limit_bytes=vmem_bytes),
        cost_estimate=pl.CostEstimate(
            flops=2 * rows * depth * width,
            bytes_accessed=2 * width * depth + 4 * rows * depth + 4 * rows * width,
            transcendentals=0,
        ),
    )(places, *pieces, weight, *after)
    return results[:chunks], [results[chunks + 5 * i : chunks + 5 * i + 5] for i in range(chunks)]


def weight_kernel(cuts, count, places, *refs):
    pieces, chunks = refs[:count], refs[count : count + len(cuts)]
    result, held = refs[-2:]
    total = None
    for chunk, cut in zip(chunks, cuts):
        at = 0
        for place, (piece, first, rows) in enumerate(cut):
            if count == 1:
                first = pl.multiple_of(places[place] + first, rows)
            held[at : at + rows, :] = pieces[piece][pl.ds(first, rows), :]
            at += rows
        term = trans_dot(held[:at, :], chunk[...])
        total = term if total is None else total + term
    result[0] = total.astype(result.dtype)


def weight_grad(places, pieces, cuts, chunks, after=(), tile=256):
    height = pieces[0].shape[1]
    width = chunks[0].shape[1]
    sizes = [chunk.shape[0] for chunk in chunks]
    return pl.pallas_call(
        functools.partial(weight_kernel, cuts, len(pieces)),
        grid_spec=pltpu.PrefetchScalarGridSpec(
            num_scalar_prefetch=1,
            grid=(height // tile,),
            in_specs=[columns(piece.shape[0], tile) for piece in pieces]
            + [whole(chunk.shape) for chunk in chunks]
            + [pl.BlockSpec(memory_space=pl.ANY)] * len(after),
            out_specs=pl.BlockSpec((1, tile, width), lambda n, *_: (0, n, 0)),
            scratch_shapes=[pltpu.VMEM((max(sizes), tile), jnp.bfloat16)],
        ),
        out_shape=jax.ShapeDtypeStruct((1, height, width), jnp.bfloat16),
        compiler_params=pltpu.CompilerParams(vmem_limit_bytes=vmem_bytes),
        cost_estimate=pl.CostEstimate(
            flops=2 * sum(sizes) * height * width,
            bytes_accessed=2 * (sum(sizes) * (height + width) + height * width),
            transcendentals=0,
        ),
    )(places, *pieces, *chunks, *after)


def hold(block, *after):
    return lax.optimization_barrier((block,) + after)


def start_col(block):
    return along_z(block, -1), along_z(block, 2), along_z(block, 1), along_y(block)


def finish_col(block, from_up, far, from_down, beside):
    beside_up, beside_down = along_z(beside, -1), along_z(beside, 1)
    beside_far = along_y(far)
    return [block, from_up, far, from_down, beside, beside_up, beside_far, beside_down]


def gather_row(block):
    return [block, along_x(block, -1), along_x(block, 2), along_x(block, 1)]


def sum_row(block):
    return (block + along_x(block, 2)) + (along_x(block, 1) + along_x(block, -1))


def sum_col(block):
    block = (block + along_z(block, 2)) + (along_z(block, 1) + along_z(block, -1))
    return block + along_y(block)


def ring_start(along, to_next, to_last):
    return along(to_next, 1), along(to_last, -1)


def ring_go_on(along, rows, next_first, last_second, from_last, from_next):
    first = along(next_first + from_last[:rows], 1)
    second = along(last_second + from_next[rows:], -1)
    return first, second


def ring_sums(rows, own, from_last, from_next, first, second):
    return (own[:rows] + from_next[:rows]) + first, (own[rows:] + from_last[rows:]) + second


def local(inputs, cotangent, stashed, weight_in, weight_out, norm_gain):
    local_input = inputs[0]
    upstream = cotangent[0]
    hidden_pre = stashed[0]
    first_weight = weight_in[0]
    second_weight = weight_out[0]
    gains = norm_gain[0]
    width = gains.shape[0]
    feature_count = width * lax.axis_size("row")
    tokens = upstream.shape[0]
    row, col = lax.axis_index("row"), lax.axis_index("col")
    step = jnp.arange(8, dtype=jnp.int32)
    owner = (col // 4 + step // 4) % 2 * 4 + (col + step) % 4
    order = (owner // 2 - row + 4) % 4 * 2 + owner % 2
    ring_owner = (row + step // 2) % 4 * 2 + step % 2
    ring_order = (ring_owner // 4 + col // 4) % 2 * 4 + (ring_owner - col + 8) % 4

    spans, start = [], 0
    for rows in chunk_rows:
        spans.append((start, rows))
        start += rows

    begun = start_col(upstream)
    activated = gelu_parts(hidden_pre.astype(jnp.float32))[0].astype(jnp.bfloat16)
    values = local_input.astype(jnp.float32)
    sums = jnp.stack([jnp.sum(values, axis=1), jnp.sum(values * values, axis=1)])
    beside, activated = hold(begun[-1], activated)
    begun = begun[:-1] + (beside,)
    activ_right, activ_left = along_x(activated, -1), along_x(activated, 1)
    cot_pieces = finish_col(upstream, *begun)

    cot_chunks, parts = parts_of(
        hidden_kernel, order, cot_pieces, second_weight, spans, (activ_right, activ_left)
    )
    first_own, to_right, to_left, *first_near = parts[0]
    first_begun = ring_start(along_x, to_right, to_left)

    sums, first_own = hold(sums, first_own)
    sums = sum_row(sums)
    average = sums[0] / feature_count
    inv_scale = lax.rsqrt(sums[1] / feature_count - average * average + epsilon)
    standard = (values - average[:, None]) * inv_scale[:, None]
    normed = (standard * gains).astype(jnp.bfloat16)
    normed_full = lax.all_to_all(
        jnp.broadcast_to(normed[None], (8,) + normed.shape), "col", 0, 0
    ).reshape(8 * tokens, width)

    def deltas_of(span, top, bottom):
        s, r = span
        slopes = [
            gelu_parts(hidden_pre[first : first + r].astype(jnp.float32))[1]
            for first in (s, tokens + s)
        ]
        return jnp.concatenate([top * slopes[0], bottom * slopes[1]]).astype(jnp.bfloat16)

    second_own, to_right, to_left, *second_near = parts[1]
    *first_begun, to_right, to_left = hold(*first_begun, to_right, to_left)
    first_rest = ring_go_on(along_x, spans[0][1], *first_near, *first_begun)
    second_begun = ring_start(along_x, to_right, to_left)
    deltas = deltas_of(spans[0], *ring_sums(spans[0][1], first_own, *first_begun, *first_rest))
    first_pieces = gather_row(deltas)
    second_rest = ring_go_on(along_x, spans[1][1], *second_near, *second_begun)
    *second_rest, deltas, normed_full = hold(*second_rest, deltas, normed_full)
    first_pieces[0] = deltas
    deltas = deltas_of(spans[1], *ring_sums(spans[1][1], second_own, *second_begun, *second_rest))
    second_pieces = gather_row(deltas)

    (first_deltas,), (parts,) = parts_of(
        normed_kernel, ring_order, first_pieces, first_weight, [(0, spans[0][1])]
    )
    first_own, to_up, to_down, *first_near = parts
    first_begun = ring_start(along_z, to_up, to_down)
    (second_deltas,), (parts,) = parts_of(
        normed_kernel, ring_order, second_pieces, first_weight, [(0, spans[1][1])]
    )
    second_own, to_up, to_down, *second_near = parts
    second_begun = ring_start(along_z, to_up, to_down)

    activ_left, activ_right, second_deltas = hold(activ_left, activ_right, second_deltas)
    activ_top = along_x(activ_left[:tokens], 1)
    activ_bottom = along_x(activ_right[tokens:], -1)
    activ_pieces = [activated, activ_right, activ_top, activ_bottom, activ_left]

    activ_cuts, normed_cuts = [], []
    for s, r in spans:
        activ_cuts.append(
            [
                (0, s, r),
                (0, tokens + s, r),
                (1, s, r),
                (1, tokens + s, r),
                (2, s, r),
                (3, s, r),
                (4, s, r),
                (4, tokens + s, r),
            ]
        )
        normed_cuts.append([(0, s, r)] * 8)
    in_grad = weight_grad(
        owner * tokens, [normed_full], normed_cuts, [first_deltas, second_deltas]
    )
    out_grad = weight_grad(owner, activ_pieces, activ_cuts, cot_chunks)

    first_rest = ring_go_on(along_z, spans[0][1], *first_near, *first_begun)
    *second_begun, in_grad = hold(*second_begun, in_grad)
    second_rest = ring_go_on(along_z, spans[1][1], *second_near, *second_begun)
    same, other = ring_sums(spans[0][1], first_own, *first_begun, *first_rest)
    grads = [same + along_y(other)]
    *second_rest, out_grad = hold(*second_rest, out_grad)
    same, other = ring_sums(spans[1][1], second_own, *second_begun, *second_rest)
    grads.append(same + along_y(other))

    normed_grad = jnp.concatenate(grads)
    gain_part = jnp.sum(normed_grad * standard, axis=0)
    scaled_grad = normed_grad * gains
    means = jnp.stack([jnp.sum(scaled_grad, axis=1), jnp.sum(scaled_grad * standard, axis=1)])
    means = sum_row(means) / feature_count
    means, gain_part = hold(means, gain_part)
    result_grad = upstream.astype(jnp.float32) + inv_scale[:, None] * (
        scaled_grad - means[0][:, None] - standard * means[1][:, None]
    )
    received = to_layer_before(result_grad.astype(jnp.bfloat16))
    gain_grad = sum_col(gain_part[None])
    return (in_grad, out_grad, gain_grad, received[None])


def solution(mesh):
    return jax.shard_map(
        local,
        mesh=mesh,
        in_specs=(
            P("section", "col", "row"),
            P("section", "col", "row"),
            P("section", "row", "col"),
            P("section", "row", "col"),
            P("section", "col", "row"),
            P("section", "row"),
        ),
        out_specs=(
            P("section", "row", "col"),
            P("section", "col", "row"),
            P("section", "row"),
            P("section", "col", "row"),
        ),
        check_vma=False,
    )
```

time: 422 us -> 234 us (0.55)
  waiting for transfers between devices: 319 us -> 88.9 us
  starting transfers between devices: 5.39 us -> 77.7 us
  Pallas kernels: 0 us -> 46.6 us
  matrix products: 37.9 us -> 0 us
  blocking collectives: 36.7 us -> 0 us
  between operations: 14.1 us -> 1.06 us
  other arithmetic: 7.43 us -> 13.1 us
  local copies, waits for them, and re-layouts: 1.08 us -> 6.14 us
    all_gather x4 -> x0, waiting for transfers between devices: 165 us -> none  [the longest x1 68 us: local(): grad_full = lax.all_gather(upstream, 'col', axis=0, tiled=True)]
    reduce_scatter x2 -> x0, waiting for transfers between devices: 152 us -> none  [the longest x1 90.3 us: local(): lax.psum_scatter(times_trans(delta_full, first_weight), 'col', scatter_di...]
    ppermute x1 -> x46, waiting for transfers between devices: 0.01 us -> 88.9 us  [the longest x24 49.3 us: along_x(): return lax.ppermute(block, 'row', [(i, (i + step) % 4) for i in range(4)])]
    ppermute x1 -> x46, starting transfers between devices: 5.15 us -> 72.3 us  [the longest x16 25.4 us: along_z(): return lax.ppermute(block, 'col', route)]
    pallas_call x0 -> x5, Pallas kernels: none -> 46.6 us  [the longest x3 25.4 us: parts_of(): pl.pallas_call(functools.partial(kernel, spans, tile, len(after)), grid_s...]
    dot_general x4 -> x0, matrix products: 37.9 us -> none  [the longest x2 19.6 us: times_trans(): lax.dot_general(left, right, (((1,), (1,)), ((), ())), preferred_element_...]
    psum x3 -> x0, blocking collectives: 36.7 us -> none  [the longest x1 21.7 us: local(): gain_grad = lax.psum(jnp.sum(normed_grad * standard, axis=0), 'col')]
    add x0 -> x16, other arithmetic: none -> 7.38 us  [the longest x4 3.02 us: ring_go_on(): second = along(last_second + from_next[rows:], -1)]
  transfers between devices with their start and end apart: 7 -> 47, of which waited for: 6 -> 25; matrix products, arithmetic and copies ran while one was open for 3% -> 7% of each run, Pallas kernels for 0% -> 15%
where the time goes in v2:
time: 234 us
  waiting for transfers between devices  88.9 us (38%)
  starting transfers between devices  77.7 us (33%)
  Pallas kernels  46.6 us (20%)
  other arithmetic  13.1 us (6%)
  local copies, waits for them, and re-layouts  6.14 us (3%)
    ppermute x24, waiting for transfers between devices, along_x(): return lax.ppermute(block, 'row', [(i, (i + step) % 4) for i in range(4)])  49.3 us
    pallas_call x3, Pallas kernels, parts_of(): pl.pallas_call(functools.partial(kernel, spans, tile, len(after)), grid_s...  25.4 us
    ppermute x16, starting transfers between devices, along_z(): return lax.ppermute(block, 'col', route)  25.4 us
    ppermute x16, waiting for transfers between devices, along_z(): return lax.ppermute(block, 'col', route)  25.2 us
    ppermute x24, starting transfers between devices, along_x(): return lax.ppermute(block, 'row', [(i, (i + step) % 4) for i in range(4)])  24.3 us
    pallas_call x2, Pallas kernels, weight_grad(): pl.pallas_call(functools.partial(weight_kernel, cuts, len(pieces)), grid_...  21.2 us
    ppermute x1, starting transfers between devices, to_layer_before(): return lax.ppermute(block, 'section', [(i, i - 1) for i in range(1, 4)])  18.2 us
    ppermute x5, waiting for transfers between devices, along_y(): return lax.ppermute(block, 'col', [(j, (j + 4) % 8) for j in range(8)])  13.5 us
  transfers between devices with their start and end apart: 47, of which 25 were waited for; matrix products, arithmetic and copies ran while one was open for 7% of the time, Pallas kernels for 15%

profile of v2, /device:TPU:1, one launch (start us, length us, event | category | flops | bytes accessed | tf_op | source)
XLA Modules:
  0.0 233.5 jit_solution(620682042950146885)
XLA Ops:
  0.6 3.8 %collective-permute-start.3 = (bf16[128,1536]{1,0:T(8,128)(2,1)}, bf16[128,1536]{1,0:T(8,128)(2,1)S(1)}, u32[]{:S(2)}, u32[]{:S(2)}) collective-permute-start(bf16[128,1536]{1,0:T(8,128)(2,1)} %bitcast.70), channel_id=1, source_target_pairs={{0,4},{1,5},{2,6},{3,7},{4,0},{5,1},{6,2},{7,3},{8,12},{9,13},{10,... | collective-permute-start | bytes 1179656 | tf_op jit(solution)/shard_map/ppermute | solution.py:28
  4.5 3.6 %collective-permute-start.1 = (bf16[128,1536]{1,0:T(8,128)(2,1)}, bf16[128,1536]{1,0:T(8,128)(2,1)S(1)}, u32[]{:S(2)}, u32[]{:S(2)}) collective-permute-start(bf16[128,1536]{1,0:T(8,128)(2,1)} %bitcast.71), channel_id=1, source_target_pairs={{0,2},{1,3},{2,0},{3,1},{4,6},{5,7},{6,4},{7,5},{8,10},{9,11},{10,... | collective-permute-start | bytes 1179656 | tf_op jit(solution)/shard_map/ppermute | solution.py:24
  16.9 3.0 %collective-permute-start.4 = (bf16[128,1536]{1,0:T(8,128)(2,1)S(1)}, bf16[128,1536]{1,0:T(8,128)(2,1)S(1)}, u32[]{:S(2)}, u32[]{:S(2)}) collective-permute-start(bf16[128,1536]{1,0:T(8,128)(2,1)S(1)} %collective-permute-done.3.refs_4_), channel_id=1, source_target_pairs={{0,3},{1,0},{2,1},{3,2},{4,7},{5,4},{6,5},{7,6},{8,11},{9,8},{10,9... | collective-permute-start | bytes 1179656 | tf_op jit(solution)/shard_map/ppermute | solution.py:24
  19.9 6.2 %collective-permute-done.refs_1_ = bf16[128,1536]{1,0:T(8,128)(2,1)} collective-permute-done((bf16[128,1536]{1,0:T(8,128)(2,1)}, bf16[128,1536]{1,0:T(8,128)(2,1)}, u32[]{:S(2)}, u32[]{:S(2)}) %collective-permute-start) | collective-permute-done | bytes 393248 | tf_op jit(solution)/shard_map/ppermute | solution.py:24
  28.5 5.8 %collective-permute-done.4.refs_5_ = bf16[128,1536]{1,0:T(8,128)(2,1)S(1)} collective-permute-done((bf16[128,1536]{1,0:T(8,128)(2,1)S(1)}, bf16[128,1536]{1,0:T(8,128)(2,1)S(1)}, u32[]{:S(2)}, u32[]{:S(2)}) %collective-permute-start.4) | collective-permute-done | bytes 393248 | tf_op jit(solution)/shard_map/ppermute | solution.py:24
  39.4 10.5 %shard_map.93 = (bf16[512,1536]{1,0:T(8,128)(2,1)}, bf16[512,1536]{1,0:T(8,128)(2,1)}, f32[128,1536]{1,0:T(8,128)}, f32[128,1536]{1,0:T(8,128)}, f32[128,1536]{1...) custom-call(s32[8]{0:T(128)} %fusion.61.places, ...), custom_call_target="tpu_custom_call" | custom-call | flops 4831838208 | bytes 17301504 | tf_op jit(solution)/shard_map/pallas_call | solution.py:166
  50.0 2.8 %collective-permute-start.17 = (f32[2,128]{1,0:T(2,128)S(1)}, f32[2,128]{1,0:T(2,128)S(1)}, u32[]{:S(2)}, u32[]{:S(2)}) collective-permute-start(f32[2,128]{1,0:T(2,128)S(1)} %pad_maximum_fusion.3), channel_id=1, source_target_pairs={{0,16},{8,24},{16,0},{24,8},{1,17},{9,25},{17,1},{25,9},{2,18},{10... | collective-permute-start | bytes 3080 | tf_op jit(solution)/shard_map/ppermute | solution.py:19
  59.4 5.5 %all-to-all-start = ((bf16[8,128,1536]{2,1,0:T(8,128)(2,1)}), bf16[8,128,1536]{2,1,0:T(8,128)(2,1)}, u32[]{:S(2)}, u32[]{:S(2)}) async-start(bf16[8,128,1536]{2,1,0:T(8,128)(2,1)} %broadcast_in_dim.18), calls=%async_computation | async-start | bytes 6291456 | tf_op jit(solution)/shard_map/all_to_all | solution.py:318
  64.8 6.6 %collective-permute-done.10 = f32[128,1536]{1,0:T(8,128)S(1)} collective-permute-done((f32[128,1536]{1,0:T(8,128)}, f32[128,1536]{1,0:T(8,128)S(1)}, u32[]{:S(2)}, u32[]{:S(2)}) %collective-permute-start.10) | collective-permute-done | bytes 786464 | tf_op jit(solution)/shard_map/ppermute | solution.py:19
  77.0 10.7 %collective-permute-done.11 = f32[128,1536]{1,0:T(8,128)S(1)} collective-permute-done((f32[128,1536]{1,0:T(8,128)}, f32[128,1536]{1,0:T(8,128)S(1)}, u32[]{:S(2)}, u32[]{:S(2)}) %collective-permute-start.11) | collective-permute-done | bytes 786464 | tf_op jit(solution)/shard_map/ppermute | solution.py:19
  90.7 5.5 %collective-permute-done.16 = f32[64,1536]{1,0:T(8,128)S(1)} collective-permute-done((f32[64,1536]{1,0:T(8,128)S(1)}, f32[64,1536]{1,0:T(8,128)S(1)}, u32[]{:S(2)}, u32[]{:S(2)}) %collective-permute-start.16) | collective-permute-done | bytes 393248 | tf_op jit(solution)/shard_map/ppermute | solution.py:19
  100.4 4.1 %collective-permute-done.14 = f32[64,1536]{1,0:T(8,128)} collective-permute-done((f32[64,1536]{1,0:T(8,128)S(1)}, f32[64,1536]{1,0:T(8,128)}, u32[]{:S(2)}, u32[]{:S(2)}) %collective-permute-start.14) | collective-permute-done | bytes 393248 | tf_op jit(solution)/shard_map/ppermute | solution.py:19
  109.9 3.1 %collective-permute-done.25.refs_1_ = bf16[128,1536]{1,0:T(8,128)(2,1)} collective-permute-done((bf16[128,1536]{1,0:T(8,128)(2,1)S(1)}, bf16[128,1536]{1,0:T(8,128)(2,1)}, u32[]{:S(2)}, u32[]{:S(2)}) %collective-permute-start.25) | collective-permute-done | bytes 393248 | tf_op jit(solution)/shard_map/ppermute | solution.py:19
  113.9 6.8 %collective-permute-done.27.refs_3_ = bf16[128,1536]{1,0:T(8,128)(2,1)} collective-permute-done((bf16[128,1536]{1,0:T(8,128)(2,1)S(1)}, bf16[128,1536]{1,0:T(8,128)(2,1)}, u32[]{:S(2)}, u32[]{:S(2)}) %collective-permute-start.27) | collective-permute-done | bytes 393248 | tf_op jit(solution)/shard_map/ppermute | solution.py:19
  120.7 7.4 %shard_map.95 = (bf16[512,1536]{1,0:T(8,128)(2,1)}, f32[128,1536]{1,0:T(8,128)}, f32[128,1536]{1,0:T(8,128)}, f32[128,1536]{1,0:T(8,128)}, f32[64,1536]{1,0:T(8,128)}, /*index=5*/f32[64,1536]{1,0:T(8,128)}) custom-call(s32[8]{0:T(128)} %fusion.59.places, bf16[128,1536]{1,0:T(8,128)(2,1)} %copy-done.7, bf16[128,1536]{1,0:T(8,128)(2,1)} %collective-permute-done.25.refs_1_, ...), custom_call_target="tpu_custom_call" | custom-call | flops 2415919104 | bytes 11010048 | tf_op jit(solution)/shard_map/pallas_call | solution.py:166
  130.6 5.4 %collective-permute-done.22.refs_3_ = bf16[128,1536]{1,0:T(8,128)(2,1)} collective-permute-done((bf16[128,1536]{1,0:T(8,128)(2,1)S(1)}, bf16[128,1536]{1,0:T(8,128)(2,1)}, u32[]{:S(2)}, u32[]{:S(2)}) %collective-permute-start.22) | collective-permute-done | bytes 393248 | tf_op jit(solution)/shard_map/ppermute | solution.py:19
  136.0 7.5 %shard_map.94 = (bf16[512,1536]{1,0:T(8,128)(2,1)}, f32[128,1536]{1,0:T(8,128)}, f32[128,1536]{1,0:T(8,128)}, f32[128,1536]{1,0:T(8,128)}, f32[64,1536]{1,0:T(8,128)}, /*index=5*/f32[64,1536]{1,0:T(8,128)}) custom-call(s32[8]{0:T(128)} %fusion.59.places, bf16[128,1536]{1,0:T(8,128)(2,1)} %copy-done.8, bf16[128,1536]{1,0:T(8,128)(2,1)} %collective-permute-done.20.refs_1_, ...), custom_call_target="tpu_custom_call" | custom-call | flops 2415919104 | bytes 11010048 | tf_op jit(solution)/shard_map/pallas_call | solution.py:166
  147.0 10.4 %shard_map.96 = bf16[1,1536,1536]{2,1,0:T(8,128)(2,1)} custom-call(s32[8]{0:T(128)} %get-tuple-element.101.places, bf16[1024,1536]{1,0:T(8,128)(2,1)} %bitcast.14.refs_0_, bf16[512,1536]{1,0:T(8,128)(2,1)} %get-tuple-element.75.refs_1_, bf16[512,1536]{1,0:T(8,128)(2,1)} %get-tuple-element.77.refs_2_), custom_call_target="tpu_custom_call" | custom-call | flops 4831838208 | bytes 11010048 | tf_op jit(solution)/shard_map/pallas_call | solution.py:213
  161.9 6.4 %collective-permute-start.35 = (f32[64,1536]{1,0:T(8,128)}, f32[64,1536]{1,0:T(8,128)}, u32[]{:S(2)}, u32[]{:S(2)}) collective-permute-start(f32[64,1536]{1,0:T(8,128)} %slice_add_fusion), channel_id=1, source_target_pairs={{0,3},{1,0},{2,1},{3,2},{4,7},{5,4},{6,5},{7,6},{8,11},{9,8},{10,9... | collective-permute-start | bytes 1179656 | tf_op jit(solution)/shard_map/ppermute | solution.py:24
  168.4 10.8 %shard_map.97 = bf16[1,1536,1536]{2,1,0:T(8,128)(2,1)} custom-call(s32[8]{0:T(128)} %copy-done.20, bf16[256,1536]{1,0:T(8,128)(2,1)} %copy-done.2, bf16[256,1536]{1,0:T(8,128)(2,1)} %copy-done.15, bf16[128,1536]{1,0:T(8,128)(2,1)} %collective-permute-done.30.refs_2_, bf16[128,1536]{1,0:T(8,128)(2,1)} %collective-permute-done.31.refs_3_, ...), custom_call_target="tpu_custom_call" | custom-call | flops 4831838208 | bytes 11010048 | tf_op jit(solution)/shard_map/pallas_call | solution.py:213
  183.4 8.1 %collective-permute-done.29 = f32[64,1536]{1,0:T(8,128)S(1)} collective-permute-done((f32[64,1536]{1,0:T(8,128)S(1)}, f32[64,1536]{1,0:T(8,128)S(1)}, u32[]{:S(2)}, u32[]{:S(2)}) %collective-permute-start.29) | collective-permute-done | bytes 393248 | tf_op jit(solution)/shard_map/ppermute | solution.py:24
  194.1 5.7 %collective-permute-done.37 = f32[64,1536]{1,0:T(8,128)S(1)} collective-permute-done((f32[64,1536]{1,0:T(8,128)S(1)}, f32[64,1536]{1,0:T(8,128)S(1)}, u32[]{:S(2)}, u32[]{:S(2)}) %collective-permute-start.37) | collective-permute-done | bytes 393248 | tf_op jit(solution)/shard_map/ppermute | solution.py:28
  208.7 18.2 %collective-permute-start.45 = (bf16[128,1536]{1,0:T(8,128)(2,1)S(1)}, bf16[128,1536]{1,0:T(8,128)(2,1)S(1)}, u32[]{:S(2)}, u32[]{:S(2)}) collective-permute-start(bf16[128,1536]{1,0:T(8,128)(2,1)S(1)} %fusion.16), channel_id=1, source_target_pairs={{32,0},{64,32},{96,64},{33,1},{65,33},{97,65},{34,2},{66,34},{98,6... | collective-permute-start | bytes 1179656 | tf_op jit(solution)/shard_map/ppermute | solution.py:32
  227.2 4.0 %collective-permute-done.44 = f32[1,1536]{1,0:T(1,128)S(1)} collective-permute-done((f32[1,1536]{1,0:T(1,128)S(1)}, f32[1,1536]{1,0:T(1,128)S(1)}, u32[]{:S(2)}, u32[]{:S(2)}) %collective-permute-start.44) | collective-permute-done | bytes 6176 | tf_op jit(solution)/shard_map/ppermute | solution.py:28
  (166 shorter events, 70.5 us)
Async XLA Ops:
  8.1 18.0 %collective-permute-start = (bf16[128,1536]{1,0:T(8,128)(2,1)}, bf16[128,1536]{1,0:T(8,128)(2,1)}, u32[]{:S(2)}, u32[]{:S(2)}) collective-permute-start(bf16[128,1536]{1,0:T(8,128)(2,1)} %bitcast.72), channel_id=1, source_target_pairs={{0,3},{1,0},{2,1},{3,2},{4,7},{5,4},{6,5},{7,6},{8,11},{9,8},{10,9... | collective-permute-start | bytes 1179656 | tf_op jit(solution)/shard_map/ppermute | solution.py:24
  8.5 18.9 %collective-permute-start.2 = (bf16[128,1536]{1,0:T(8,128)(2,1)}, bf16[128,1536]{1,0:T(8,128)(2,1)}, u32[]{:S(2)}, u32[]{:S(2)}) collective-permute-start(bf16[128,1536]{1,0:T(8,128)(2,1)} %bitcast.73), channel_id=1, source_target_pairs={{0,1},{1,2},{2,3},{3,0},{4,5},{5,6},{6,7},{7,4},{8,9},{9,10},{10,1... | collective-permute-start | bytes 1179656 | tf_op jit(solution)/shard_map/ppermute | solution.py:24
  13.2 24.6 %collective-permute-start.7 = (bf16[256,1536]{1,0:T(8,128)(2,1)S(1)}, bf16[256,1536]{1,0:T(8,128)(2,1)S(1)}, u32[]{:S(2)}, u32[]{:S(2)}) collective-permute-start(bf16[256,1536]{1,0:T(8,128)(2,1)S(1)} %fusion.3.refs_0_), channel_id=1, source_target_pairs={{0,24},{8,0},{16,8},{24,16},{1,25},{9,1},{17,9},{25,17},{2,26},{10... | collective-permute-start | bytes 2359304 | tf_op jit(solution)/shard_map/ppermute | solution.py:19
  15.7 22.1 %collective-permute-start.8 = (bf16[256,1536]{1,0:T(8,128)(2,1)S(1)}, bf16[256,1536]{1,0:T(8,128)(2,1)S(1)}, u32[]{:S(2)}, u32[]{:S(2)}) collective-permute-start(bf16[256,1536]{1,0:T(8,128)(2,1)S(1)} %fusion.3.refs_0_), channel_id=1, source_target_pairs={{0,8},{8,16},{16,24},{24,0},{1,9},{9,17},{17,25},{25,1},{2,10},{10... | collective-permute-start | bytes 2359304 | tf_op jit(solution)/shard_map/ppermute | solution.py:19
  16.9 17.5 %collective-permute-start.4 = (bf16[128,1536]{1,0:T(8,128)(2,1)S(1)}, bf16[128,1536]{1,0:T(8,128)(2,1)S(1)}, u32[]{:S(2)}, u32[]{:S(2)}) collective-permute-start(bf16[128,1536]{1,0:T(8,128)(2,1)S(1)} %collective-permute-done.3.refs_4_), channel_id=1, source_target_pairs={{0,3},{1,0},{2,1},{3,2},{4,7},{5,4},{6,5},{7,6},{8,11},{9,8},{10,9... | collective-permute-start | bytes 1179656 | tf_op jit(solution)/shard_map/ppermute | solution.py:24
  55.6 17.1 %collective-permute-start.9 = (f32[128,1536]{1,0:T(8,128)}, f32[128,1536]{1,0:T(8,128)S(1)}, u32[]{:S(2)}, u32[]{:S(2)}) collective-permute-start(f32[128,1536]{1,0:T(8,128)} %get-tuple-element.54), channel_id=1, source_target_pairs={{0,8},{8,16},{16,24},{24,0},{1,9},{9,17},{17,25},{25,1},{2,10},{10... | collective-permute-start | bytes 2359304 | tf_op jit(solution)/shard_map/ppermute | solution.py:19
  59.4 46.9 %all-to-all-start = ((bf16[8,128,1536]{2,1,0:T(8,128)(2,1)}), bf16[8,128,1536]{2,1,0:T(8,128)(2,1)}, u32[]{:S(2)}, u32[]{:S(2)}) async-start(bf16[8,128,1536]{2,1,0:T(8,128)(2,1)} %broadcast_in_dim.18), calls=%async_computation | async-start | bytes 6291456 | tf_op jit(solution)/shard_map/all_to_all | solution.py:318
  73.0 23.1 %collective-permute-start.16 = (f32[64,1536]{1,0:T(8,128)S(1)}, f32[64,1536]{1,0:T(8,128)S(1)}, u32[]{:S(2)}, u32[]{:S(2)}) collective-permute-start(f32[64,1536]{1,0:T(8,128)S(1)} %slice_add_fusion.10), channel_id=1, source_target_pairs={{0,24},{8,0},{16,8},{24,16},{1,25},{9,1},{17,9},{25,17},{2,26},{10... | collective-permute-start | bytes 1179656 | tf_op jit(solution)/shard_map/ppermute | solution.py:19
  75.7 21.9 %collective-permute-start.15 = (f32[64,1536]{1,0:T(8,128)S(1)}, f32[64,1536]{1,0:T(8,128)S(1)}, u32[]{:S(2)}, u32[]{:S(2)}) collective-permute-start(f32[64,1536]{1,0:T(8,128)S(1)} %slice_add_fusion.11), channel_id=1, source_target_pairs={{0,8},{8,16},{16,24},{24,0},{1,9},{9,17},{17,25},{25,1},{2,10},{10... | collective-permute-start | bytes 1179656 | tf_op jit(solution)/shard_map/ppermute | solution.py:19
  100.0 20.6 %collective-permute-start.27 = (bf16[128,1536]{1,0:T(8,128)(2,1)S(1)}, bf16[128,1536]{1,0:T(8,128)(2,1)}, u32[]{:S(2)}, u32[]{:S(2)}) collective-permute-start(bf16[128,1536]{1,0:T(8,128)(2,1)S(1)} %pad_maximum_fusion.1.refs_0_), channel_id=1, source_target_pairs={{0,8},{8,16},{16,24},{24,0},{1,9},{9,17},{17,25},{25,1},{2,10},{10... | collective-permute-start | bytes 1179656 | tf_op jit(solution)/shard_map/ppermute | solution.py:19
  108.2 21.4 %collective-permute-start.20 = (bf16[128,1536]{1,0:T(8,128)(2,1)S(1)}, bf16[128,1536]{1,0:T(8,128)(2,1)}, u32[]{:S(2)}, u32[]{:S(2)}) collective-permute-start(bf16[128,1536]{1,0:T(8,128)(2,1)S(1)} %pad_maximum_fusion.2.refs_0_), channel_id=1, source_target_pairs={{0,24},{8,0},{16,8},{24,16},{1,25},{9,1},{17,9},{25,17},{2,26},{10... | collective-permute-start | bytes 1179656 | tf_op jit(solution)/shard_map/ppermute | solution.py:19
  108.3 22.3 %collective-permute-start.21 = (bf16[128,1536]{1,0:T(8,128)(2,1)S(1)}, bf16[128,1536]{1,0:T(8,128)(2,1)}, u32[]{:S(2)}, u32[]{:S(2)}) collective-permute-start(bf16[128,1536]{1,0:T(8,128)(2,1)S(1)} %pad_maximum_fusion.2.refs_0_), channel_id=1, source_target_pairs={{0,16},{8,24},{16,0},{24,8},{1,17},{9,25},{17,1},{25,9},{2,18},{10... | collective-permute-start | bytes 1179656 | tf_op jit(solution)/shard_map/ppermute | solution.py:19
  113.0 23.0 %collective-permute-start.22 = (bf16[128,1536]{1,0:T(8,128)(2,1)S(1)}, bf16[128,1536]{1,0:T(8,128)(2,1)}, u32[]{:S(2)}, u32[]{:S(2)}) collective-permute-start(bf16[128,1536]{1,0:T(8,128)(2,1)S(1)} %pad_maximum_fusion.2.refs_0_), channel_id=1, source_target_pairs={{0,8},{8,16},{16,24},{24,0},{1,9},{9,17},{17,25},{25,1},{2,10},{10... | collective-permute-start | bytes 1179656 | tf_op jit(solution)/shard_map/ppermute | solution.py:19
  128.1 29.4 %collective-permute-start.32 = (f32[128,1536]{1,0:T(8,128)}, f32[128,1536]{1,0:T(8,128)S(1)}, u32[]{:S(2)}, u32[]{:S(2)}) collective-permute-start(f32[128,1536]{1,0:T(8,128)} %get-tuple-element.89), channel_id=1, source_target_pairs={{0,3},{1,0},{2,1},{3,2},{4,7},{5,4},{6,5},{7,6},{8,11},{9,8},{10,9... | collective-permute-start | bytes 2359304 | tf_op jit(solution)/shard_map/ppermute | solution.py:24
  129.0 52.9 %collective-permute-start.33 = (f32[128,1536]{1,0:T(8,128)}, f32[128,1536]{1,0:T(8,128)S(1)}, u32[]{:S(2)}, u32[]{:S(2)}) collective-permute-start(f32[128,1536]{1,0:T(8,128)} %get-tuple-element.91), channel_id=1, source_target_pairs={{0,1},{1,2},{2,3},{3,0},{4,5},{5,6},{6,7},{7,4},{8,9},{9,10},{10,1... | collective-permute-start | bytes 2359304 | tf_op jit(solution)/shard_map/ppermute | solution.py:24
  144.3 17.7 %collective-permute-start.30 = (bf16[128,1536]{1,0:T(8,128)(2,1)}, bf16[128,1536]{1,0:T(8,128)(2,1)}, u32[]{:S(2)}, u32[]{:S(2)}) collective-permute-start(bf16[128,1536]{1,0:T(8,128)(2,1)} %slice.126), channel_id=1, source_target_pairs={{0,8},{8,16},{16,24},{24,0},{1,9},{9,17},{17,25},{25,1},{2,10},{10... | collective-permute-start | bytes 1179656 | tf_op jit(solution)/shard_map/ppermute | solution.py:19
  146.6 21.8 %collective-permute-start.31 = (bf16[128,1536]{1,0:T(8,128)(2,1)S(1)}, bf16[128,1536]{1,0:T(8,128)(2,1)}, u32[]{:S(2)}, u32[]{:S(2)}) collective-permute-start(bf16[128,1536]{1,0:T(8,128)(2,1)S(1)} %slice.127), channel_id=1, source_target_pairs={{0,24},{8,0},{16,8},{24,16},{1,25},{9,1},{17,9},{25,17},{2,26},{10... | collective-permute-start | bytes 1179656 | tf_op jit(solution)/shard_map/ppermute | solution.py:19
  147.0 32.1 %collective-permute-start.23 = (f32[128,1536]{1,0:T(8,128)}, f32[128,1536]{1,0:T(8,128)S(1)}, u32[]{:S(2)}, u32[]{:S(2)}) collective-permute-start(f32[128,1536]{1,0:T(8,128)} %get-tuple-element.71), channel_id=1, source_target_pairs={{0,1},{1,2},{2,3},{3,0},{4,5},{5,6},{6,7},{7,4},{8,9},{9,10},{10,1... | collective-permute-start | bytes 2359304 | tf_op jit(solution)/shard_map/ppermute | solution.py:24
  157.5 21.7 %collective-permute-start.24 = (f32[128,1536]{1,0:T(8,128)}, f32[128,1536]{1,0:T(8,128)S(1)}, u32[]{:S(2)}, u32[]{:S(2)}) collective-permute-start(f32[128,1536]{1,0:T(8,128)} %get-tuple-element.72), channel_id=1, source_target_pairs={{0,3},{1,0},{2,1},{3,2},{4,7},{5,4},{6,5},{7,6},{8,11},{9,8},{10,9... | collective-permute-start | bytes 2359304 | tf_op jit(solution)/shard_map/ppermute | solution.py:24
  161.9 20.0 %collective-permute-start.35 = (f32[64,1536]{1,0:T(8,128)}, f32[64,1536]{1,0:T(8,128)}, u32[]{:S(2)}, u32[]{:S(2)}) collective-permute-start(f32[64,1536]{1,0:T(8,128)} %slice_add_fusion), channel_id=1, source_target_pairs={{0,3},{1,0},{2,1},{3,2},{4,7},{5,4},{6,5},{7,6},{8,11},{9,8},{10,9... | collective-permute-start | bytes 1179656 | tf_op jit(solution)/shard_map/ppermute | solution.py:24
  204.7 22.3 %collective-permute-start.41 = (f32[1,1536]{1,0:T(1,128)S(1)}, f32[1,1536]{1,0:T(1,128)S(1)}, u32[]{:S(2)}, u32[]{:S(2)}) collective-permute-start(f32[1,1536]{1,0:T(1,128)S(1)} %broadcast_in_dim.19), channel_id=1, source_target_pairs={{0,2},{1,3},{2,0},{3,1},{4,6},{5,7},{6,4},{7,5},{8,10},{9,11},{10,... | collective-permute-start | bytes 18440 | tf_op jit(solution)/shard_map/ppermute | solution.py:24
  205.7 21.3 %collective-permute-start.42 = (f32[1,1536]{1,0:T(1,128)S(1)}, f32[1,1536]{1,0:T(1,128)S(1)}, u32[]{:S(2)}, u32[]{:S(2)}) collective-permute-start(f32[1,1536]{1,0:T(1,128)S(1)} %broadcast_in_dim.19), channel_id=1, source_target_pairs={{0,1},{1,2},{2,3},{3,0},{4,5},{5,6},{6,7},{7,4},{8,9},{9,10},{10,1... | collective-permute-start | bytes 18440 | tf_op jit(solution)/shard_map/ppermute | solution.py:24
  208.1 18.9 %collective-permute-start.43 = (f32[1,1536]{1,0:T(1,128)S(1)}, f32[1,1536]{1,0:T(1,128)S(1)}, u32[]{:S(2)}, u32[]{:S(2)}) collective-permute-start(f32[1,1536]{1,0:T(1,128)S(1)} %broadcast_in_dim.19), channel_id=1, source_target_pairs={{0,3},{1,0},{2,1},{3,2},{4,7},{5,4},{6,5},{7,6},{8,11},{9,8},{10,9... | collective-permute-start | bytes 18440 | tf_op jit(solution)/shard_map/ppermute | solution.py:24
  208.7 24.0 %collective-permute-start.45 = (bf16[128,1536]{1,0:T(8,128)(2,1)S(1)}, bf16[128,1536]{1,0:T(8,128)(2,1)S(1)}, u32[]{:S(2)}, u32[]{:S(2)}) collective-permute-start(bf16[128,1536]{1,0:T(8,128)(2,1)S(1)} %fusion.16), channel_id=1, source_target_pairs={{32,0},{64,32},{96,64},{33,1},{65,33},{97,65},{34,2},{66,34},{98,6... | collective-permute-start | bytes 1179656 | tf_op jit(solution)/shard_map/ppermute | solution.py:32
  (49 other events, 578.8 us)

commit v3 on v2

--- a/solution.py
+++ b/solution.py
@@ -158,7 +158,7 @@
             save_copy(index).wait()
 
 
-def parts_of(kernel, places, pieces, weight, spans, after=(), tile=256):
+def parts_of(kernel, places, pieces, weight, spans, after=(), tile=512):
     width, depth = weight.shape
     rows = sum(8 * r for _, r in spans)
     chunks = len(spans)
@@ -206,7 +206,7 @@
     result[0] = total.astype(result.dtype)
 
 
-def weight_grad(places, pieces, cuts, chunks, after=(), tile=256):
+def weight_grad(places, pieces, cuts, chunks, after=(), tile=512):
     height = pieces[0].shape[1]
     width = chunks[0].shape[1]
     sizes = [chunk.shape[0] for chunk in chunks]

time: 234 us -> 233 us (level)
  Pallas kernels: 46.6 us -> 43.8 us
  transfers between devices with their start and end apart: 47 -> 47, of which waited for: 25 -> 25; matrix products, arithmetic and copies ran while one was open for 7% -> 7% of each run, Pallas kernels for 15% -> 14%
where the time goes in v3:
time: 233 us; the launch traced here: 232 us
  waiting for transfers between devices  88.6 us (38%)
  starting transfers between devices  79.5 us (34%)
  Pallas kernels  43.8 us (19%)
  other arithmetic  13.1 us (6%)
  local copies, waits for them, and re-layouts  6.14 us (3%)
    ppermute x24, waiting for transfers between devices, along_x(): return lax.ppermute(block, 'row', [(i, (i + step) % 4) for i in range(4)])  50 us
    ppermute x16, starting transfers between devices, along_z(): return lax.ppermute(block, 'col', route)  26.3 us
    pallas_call x3, Pallas kernels, parts_of(): pl.pallas_call(functools.partial(kernel, spans, tile, len(after)), grid_s...  24.3 us
    ppermute x24, starting transfers between devices, along_x(): return lax.ppermute(block, 'row', [(i, (i + step) % 4) for i in range(4)])  24.2 us
    ppermute x16, waiting for transfers between devices, along_z(): return lax.ppermute(block, 'col', route)  24.2 us
    pallas_call x2, Pallas kernels, weight_grad(): pl.pallas_call(functools.partial(weight_kernel, cuts, len(pieces)), grid_...  19.5 us
    ppermute x1, starting transfers between devices, to_layer_before(): return lax.ppermute(block, 'section', [(i, i - 1) for i in range(1, 4)])  19.1 us
    ppermute x5, waiting for transfers between devices, along_y(): return lax.ppermute(block, 'col', [(j, (j + 4) % 8) for j in range(8)])  13.5 us
  transfers between devices with their start and end apart: 47, of which 25 were waited for; matrix products, arithmetic and copies ran while one was open for 7% of the time, Pallas kernels for 14%

profile of v3, /device:TPU:1, one launch (start us, length us, event | category | flops | bytes accessed | tf_op | source)
XLA Modules:
  0.0 232.1 jit_solution(15119719307644937428)
XLA Ops:
  0.6 3.8 %collective-permute-start.3 = (bf16[128,1536]{1,0:T(8,128)(2,1)}, bf16[128,1536]{1,0:T(8,128)(2,1)S(1)}, u32[]{:S(2)}, u32[]{:S(2)}) collective-permute-start(bf16[128,1536]{1,0:T(8,128)(2,1)} %bitcast.70), channel_id=1, source_target_pairs={{0,4},{1,5},{2,6},{3,7},{4,0},{5,1},{6,2},{7,3},{8,12},{9,13},{10,... | collective-permute-start | bytes 1179656 | tf_op jit(solution)/shard_map/ppermute | solution.py:28
  4.5 3.6 %collective-permute-start.1 = (bf16[128,1536]{1,0:T(8,128)(2,1)}, bf16[128,1536]{1,0:T(8,128)(2,1)S(1)}, u32[]{:S(2)}, u32[]{:S(2)}) collective-permute-start(bf16[128,1536]{1,0:T(8,128)(2,1)} %bitcast.71), channel_id=1, source_target_pairs={{0,2},{1,3},{2,0},{3,1},{4,6},{5,7},{6,4},{7,5},{8,10},{9,11},{10,... | collective-permute-start | bytes 1179656 | tf_op jit(solution)/shard_map/ppermute | solution.py:24
  16.9 3.0 %collective-permute-start.4 = (bf16[128,1536]{1,0:T(8,128)(2,1)S(1)}, bf16[128,1536]{1,0:T(8,128)(2,1)S(1)}, u32[]{:S(2)}, u32[]{:S(2)}) collective-permute-start(bf16[128,1536]{1,0:T(8,128)(2,1)S(1)} %collective-permute-done.3.refs_4_), channel_id=1, source_target_pairs={{0,3},{1,0},{2,1},{3,2},{4,7},{5,4},{6,5},{7,6},{8,11},{9,8},{10,9... | collective-permute-start | bytes 1179656 | tf_op jit(solution)/shard_map/ppermute | solution.py:24
  19.9 6.2 %collective-permute-done.refs_1_ = bf16[128,1536]{1,0:T(8,128)(2,1)} collective-permute-done((bf16[128,1536]{1,0:T(8,128)(2,1)}, bf16[128,1536]{1,0:T(8,128)(2,1)}, u32[]{:S(2)}, u32[]{:S(2)}) %collective-permute-start) | collective-permute-done | bytes 393248 | tf_op jit(solution)/shard_map/ppermute | solution.py:24
  28.5 5.8 %collective-permute-done.4.refs_5_ = bf16[128,1536]{1,0:T(8,128)(2,1)S(1)} collective-permute-done((bf16[128,1536]{1,0:T(8,128)(2,1)S(1)}, bf16[128,1536]{1,0:T(8,128)(2,1)S(1)}, u32[]{:S(2)}, u32[]{:S(2)}) %collective-permute-start.4) | collective-permute-done | bytes 393248 | tf_op jit(solution)/shard_map/ppermute | solution.py:24
  39.4 10.4 %shard_map.93 = (bf16[512,1536]{1,0:T(8,128)(2,1)}, bf16[512,1536]{1,0:T(8,128)(2,1)}, f32[128,1536]{1,0:T(8,128)}, f32[128,1536]{1,0:T(8,128)}, f32[128,1536]{1...) custom-call(s32[8]{0:T(128)} %fusion.61.places, ...), custom_call_target="tpu_custom_call" | custom-call | flops 4831838208 | bytes 17301504 | tf_op jit(solution)/shard_map/pallas_call | solution.py:166
  49.8 2.8 %collective-permute-start.17 = (f32[2,128]{1,0:T(2,128)S(1)}, f32[2,128]{1,0:T(2,128)S(1)}, u32[]{:S(2)}, u32[]{:S(2)}) collective-permute-start(f32[2,128]{1,0:T(2,128)S(1)} %pad_maximum_fusion.3), channel_id=1, source_target_pairs={{0,16},{8,24},{16,0},{24,8},{1,17},{9,25},{17,1},{25,9},{2,18},{10... | collective-permute-start | bytes 3080 | tf_op jit(solution)/shard_map/ppermute | solution.py:19
  59.2 5.5 %all-to-all-start = ((bf16[8,128,1536]{2,1,0:T(8,128)(2,1)}), bf16[8,128,1536]{2,1,0:T(8,128)(2,1)}, u32[]{:S(2)}, u32[]{:S(2)}) async-start(bf16[8,128,1536]{2,1,0:T(8,128)(2,1)} %broadcast_in_dim.18), calls=%async_computation | async-start | bytes 6291456 | tf_op jit(solution)/shard_map/all_to_all | solution.py:318
  64.6 6.6 %collective-permute-done.10 = f32[128,1536]{1,0:T(8,128)S(1)} collective-permute-done((f32[128,1536]{1,0:T(8,128)}, f32[128,1536]{1,0:T(8,128)S(1)}, u32[]{:S(2)}, u32[]{:S(2)}) %collective-permute-start.10) | collective-permute-done | bytes 786464 | tf_op jit(solution)/shard_map/ppermute | solution.py:19
  76.8 10.7 %collective-permute-done.11 = f32[128,1536]{1,0:T(8,128)S(1)} collective-permute-done((f32[128,1536]{1,0:T(8,128)}, f32[128,1536]{1,0:T(8,128)S(1)}, u32[]{:S(2)}, u32[]{:S(2)}) %collective-permute-start.11) | collective-permute-done | bytes 786464 | tf_op jit(solution)/shard_map/ppermute | solution.py:19
  90.5 5.5 %collective-permute-done.16 = f32[64,1536]{1,0:T(8,128)S(1)} collective-permute-done((f32[64,1536]{1,0:T(8,128)S(1)}, f32[64,1536]{1,0:T(8,128)S(1)}, u32[]{:S(2)}, u32[]{:S(2)}) %collective-permute-start.16) | collective-permute-done | bytes 393248 | tf_op jit(solution)/shard_map/ppermute | solution.py:19
  100.2 4.1 %collective-permute-done.14 = f32[64,1536]{1,0:T(8,128)} collective-permute-done((f32[64,1536]{1,0:T(8,128)S(1)}, f32[64,1536]{1,0:T(8,128)}, u32[]{:S(2)}, u32[]{:S(2)}) %collective-permute-start.14) | collective-permute-done | bytes 393248 | tf_op jit(solution)/shard_map/ppermute | solution.py:19
  109.7 3.1 %collective-permute-done.25.refs_1_ = bf16[128,1536]{1,0:T(8,128)(2,1)} collective-permute-done((bf16[128,1536]{1,0:T(8,128)(2,1)S(1)}, bf16[128,1536]{1,0:T(8,128)(2,1)}, u32[]{:S(2)}, u32[]{:S(2)}) %collective-permute-start.25) | collective-permute-done | bytes 393248 | tf_op jit(solution)/shard_map/ppermute | solution.py:19
  113.7 6.8 %collective-permute-done.27.refs_3_ = bf16[128,1536]{1,0:T(8,128)(2,1)} collective-permute-done((bf16[128,1536]{1,0:T(8,128)(2,1)S(1)}, bf16[128,1536]{1,0:T(8,128)(2,1)}, u32[]{:S(2)}, u32[]{:S(2)}) %collective-permute-start.27) | collective-permute-done | bytes 393248 | tf_op jit(solution)/shard_map/ppermute | solution.py:19
  120.5 7.0 %shard_map.95 = (bf16[512,1536]{1,0:T(8,128)(2,1)}, f32[128,1536]{1,0:T(8,128)}, f32[128,1536]{1,0:T(8,128)}, f32[128,1536]{1,0:T(8,128)}, f32[64,1536]{1,0:T(8,128)}, /*index=5*/f32[64,1536]{1,0:T(8,128)}) custom-call(s32[8]{0:T(128)} %fusion.59.places, bf16[128,1536]{1,0:T(8,128)(2,1)} %copy-done.7, bf16[128,1536]{1,0:T(8,128)(2,1)} %collective-permute-done.25.refs_1_, ...), custom_call_target="tpu_custom_call" | custom-call | flops 2415919104 | bytes 11010048 | tf_op jit(solution)/shard_map/pallas_call | solution.py:166
  130.4 5.6 %collective-permute-done.22.refs_3_ = bf16[128,1536]{1,0:T(8,128)(2,1)} collective-permute-done((bf16[128,1536]{1,0:T(8,128)(2,1)S(1)}, bf16[128,1536]{1,0:T(8,128)(2,1)}, u32[]{:S(2)}, u32[]{:S(2)}) %collective-permute-start.22) | collective-permute-done | bytes 393248 | tf_op jit(solution)/shard_map/ppermute | solution.py:19
  136.0 6.9 %shard_map.94 = (bf16[512,1536]{1,0:T(8,128)(2,1)}, f32[128,1536]{1,0:T(8,128)}, f32[128,1536]{1,0:T(8,128)}, f32[128,1536]{1,0:T(8,128)}, f32[64,1536]{1,0:T(8,128)}, /*index=5*/f32[64,1536]{1,0:T(8,128)}) custom-call(s32[8]{0:T(128)} %fusion.59.places, bf16[128,1536]{1,0:T(8,128)(2,1)} %copy-done.8, bf16[128,1536]{1,0:T(8,128)(2,1)} %collective-permute-done.20.refs_1_, ...), custom_call_target="tpu_custom_call" | custom-call | flops 2415919104 | bytes 11010048 | tf_op jit(solution)/shard_map/pallas_call | solution.py:166
  146.5 9.6 %shard_map.96 = bf16[1,1536,1536]{2,1,0:T(8,128)(2,1)} custom-call(s32[8]{0:T(128)} %get-tuple-element.101.places, bf16[1024,1536]{1,0:T(8,128)(2,1)} %bitcast.14.refs_0_, bf16[512,1536]{1,0:T(8,128)(2,1)} %get-tuple-element.75.refs_1_, bf16[512,1536]{1,0:T(8,128)(2,1)} %get-tuple-element.77.refs_2_), custom_call_target="tpu_custom_call" | custom-call | flops 4831838208 | bytes 11010048 | tf_op jit(solution)/shard_map/pallas_call | solution.py:213
  160.6 6.3 %collective-permute-start.35 = (f32[64,1536]{1,0:T(8,128)}, f32[64,1536]{1,0:T(8,128)}, u32[]{:S(2)}, u32[]{:S(2)}) collective-permute-start(f32[64,1536]{1,0:T(8,128)} %slice_add_fusion), channel_id=1, source_target_pairs={{0,3},{1,0},{2,1},{3,2},{4,7},{5,4},{6,5},{7,6},{8,11},{9,8},{10,9... | collective-permute-start | bytes 1179656 | tf_op jit(solution)/shard_map/ppermute | solution.py:24
  166.9 9.9 %shard_map.97 = bf16[1,1536,1536]{2,1,0:T(8,128)(2,1)} custom-call(s32[8]{0:T(128)} %copy-done.20, bf16[256,1536]{1,0:T(8,128)(2,1)} %copy-done.2, bf16[256,1536]{1,0:T(8,128)(2,1)} %copy-done.15, bf16[128,1536]{1,0:T(8,128)(2,1)} %collective-permute-done.30.refs_2_, bf16[128,1536]{1,0:T(8,128)(2,1)} %collective-permute-done.31.refs_3_, ...), custom_call_target="tpu_custom_call" | custom-call | flops 4831838208 | bytes 11010048 | tf_op jit(solution)/shard_map/pallas_call | solution.py:213
  182.1 7.2 %collective-permute-done.29 = f32[64,1536]{1,0:T(8,128)S(1)} collective-permute-done((f32[64,1536]{1,0:T(8,128)S(1)}, f32[64,1536]{1,0:T(8,128)S(1)}, u32[]{:S(2)}, u32[]{:S(2)}) %collective-permute-start.29) | collective-permute-done | bytes 393248 | tf_op jit(solution)/shard_map/ppermute | solution.py:24
  191.8 5.8 %collective-permute-done.37 = f32[64,1536]{1,0:T(8,128)S(1)} collective-permute-done((f32[64,1536]{1,0:T(8,128)S(1)}, f32[64,1536]{1,0:T(8,128)S(1)}, u32[]{:S(2)}, u32[]{:S(2)}) %collective-permute-start.37) | collective-permute-done | bytes 393248 | tf_op jit(solution)/shard_map/ppermute | solution.py:28
  206.4 19.1 %collective-permute-start.45 = (bf16[128,1536]{1,0:T(8,128)(2,1)S(1)}, bf16[128,1536]{1,0:T(8,128)(2,1)S(1)}, u32[]{:S(2)}, u32[]{:S(2)}) collective-permute-start(bf16[128,1536]{1,0:T(8,128)(2,1)S(1)} %fusion.16), channel_id=1, source_target_pairs={{32,0},{64,32},{96,64},{33,1},{65,33},{97,65},{34,2},{66,34},{98,6... | collective-permute-start | bytes 1179656 | tf_op jit(solution)/shard_map/ppermute | solution.py:32
  225.8 4.0 %collective-permute-done.44 = f32[1,1536]{1,0:T(1,128)S(1)} collective-permute-done((f32[1,1536]{1,0:T(1,128)S(1)}, f32[1,1536]{1,0:T(1,128)S(1)}, u32[]{:S(2)}, u32[]{:S(2)}) %collective-permute-start.44) | collective-permute-done | bytes 6176 | tf_op jit(solution)/shard_map/ppermute | solution.py:28
  (166 shorter events, 71.8 us)
Async XLA Ops:
  8.1 18.0 %collective-permute-start = (bf16[128,1536]{1,0:T(8,128)(2,1)}, bf16[128,1536]{1,0:T(8,128)(2,1)}, u32[]{:S(2)}, u32[]{:S(2)}) collective-permute-start(bf16[128,1536]{1,0:T(8,128)(2,1)} %bitcast.72), channel_id=1, source_target_pairs={{0,3},{1,0},{2,1},{3,2},{4,7},{5,4},{6,5},{7,6},{8,11},{9,8},{10,9... | collective-permute-start | bytes 1179656 | tf_op jit(solution)/shard_map/ppermute | solution.py:24
  8.5 18.9 %collective-permute-start.2 = (bf16[128,1536]{1,0:T(8,128)(2,1)}, bf16[128,1536]{1,0:T(8,128)(2,1)}, u32[]{:S(2)}, u32[]{:S(2)}) collective-permute-start(bf16[128,1536]{1,0:T(8,128)(2,1)} %bitcast.73), channel_id=1, source_target_pairs={{0,1},{1,2},{2,3},{3,0},{4,5},{5,6},{6,7},{7,4},{8,9},{9,10},{10,1... | collective-permute-start | bytes 1179656 | tf_op jit(solution)/shard_map/ppermute | solution.py:24
  13.2 24.6 %collective-permute-start.7 = (bf16[256,1536]{1,0:T(8,128)(2,1)S(1)}, bf16[256,1536]{1,0:T(8,128)(2,1)S(1)}, u32[]{:S(2)}, u32[]{:S(2)}) collective-permute-start(bf16[256,1536]{1,0:T(8,128)(2,1)S(1)} %fusion.3.refs_0_), channel_id=1, source_target_pairs={{0,24},{8,0},{16,8},{24,16},{1,25},{9,1},{17,9},{25,17},{2,26},{10... | collective-permute-start | bytes 2359304 | tf_op jit(solution)/shard_map/ppermute | solution.py:19
  15.7 22.1 %collective-permute-start.8 = (bf16[256,1536]{1,0:T(8,128)(2,1)S(1)}, bf16[256,1536]{1,0:T(8,128)(2,1)S(1)}, u32[]{:S(2)}, u32[]{:S(2)}) collective-permute-start(bf16[256,1536]{1,0:T(8,128)(2,1)S(1)} %fusion.3.refs_0_), channel_id=1, source_target_pairs={{0,8},{8,16},{16,24},{24,0},{1,9},{9,17},{17,25},{25,1},{2,10},{10... | collective-permute-start | bytes 2359304 | tf_op jit(solution)/shard_map/ppermute | solution.py:19
  16.9 17.5 %collective-permute-start.4 = (bf16[128,1536]{1,0:T(8,128)(2,1)S(1)}, bf16[128,1536]{1,0:T(8,128)(2,1)S(1)}, u32[]{:S(2)}, u32[]{:S(2)}) collective-permute-start(bf16[128,1536]{1,0:T(8,128)(2,1)S(1)} %collective-permute-done.3.refs_4_), channel_id=1, source_target_pairs={{0,3},{1,0},{2,1},{3,2},{4,7},{5,4},{6,5},{7,6},{8,11},{9,8},{10,9... | collective-permute-start | bytes 1179656 | tf_op jit(solution)/shard_map/ppermute | solution.py:24
  55.5 17.1 %collective-permute-start.9 = (f32[128,1536]{1,0:T(8,128)}, f32[128,1536]{1,0:T(8,128)S(1)}, u32[]{:S(2)}, u32[]{:S(2)}) collective-permute-start(f32[128,1536]{1,0:T(8,128)} %get-tuple-element.54), channel_id=1, source_target_pairs={{0,8},{8,16},{16,24},{24,0},{1,9},{9,17},{17,25},{25,1},{2,10},{10... | collective-permute-start | bytes 2359304 | tf_op jit(solution)/shard_map/ppermute | solution.py:19
  59.2 47.0 %all-to-all-start = ((bf16[8,128,1536]{2,1,0:T(8,128)(2,1)}), bf16[8,128,1536]{2,1,0:T(8,128)(2,1)}, u32[]{:S(2)}, u32[]{:S(2)}) async-start(bf16[8,128,1536]{2,1,0:T(8,128)(2,1)} %broadcast_in_dim.18), calls=%async_computation | async-start | bytes 6291456 | tf_op jit(solution)/shard_map/all_to_all | solution.py:318
  72.8 23.1 %collective-permute-start.16 = (f32[64,1536]{1,0:T(8,128)S(1)}, f32[64,1536]{1,0:T(8,128)S(1)}, u32[]{:S(2)}, u32[]{:S(2)}) collective-permute-start(f32[64,1536]{1,0:T(8,128)S(1)} %slice_add_fusion.10), channel_id=1, source_target_pairs={{0,24},{8,0},{16,8},{24,16},{1,25},{9,1},{17,9},{25,17},{2,26},{10... | collective-permute-start | bytes 1179656 | tf_op jit(solution)/shard_map/ppermute | solution.py:19
  75.5 22.0 %collective-permute-start.15 = (f32[64,1536]{1,0:T(8,128)S(1)}, f32[64,1536]{1,0:T(8,128)S(1)}, u32[]{:S(2)}, u32[]{:S(2)}) collective-permute-start(f32[64,1536]{1,0:T(8,128)S(1)} %slice_add_fusion.11), channel_id=1, source_target_pairs={{0,8},{8,16},{16,24},{24,0},{1,9},{9,17},{17,25},{25,1},{2,10},{10... | collective-permute-start | bytes 1179656 | tf_op jit(solution)/shard_map/ppermute | solution.py:19
  99.8 20.6 %collective-permute-start.27 = (bf16[128,1536]{1,0:T(8,128)(2,1)S(1)}, bf16[128,1536]{1,0:T(8,128)(2,1)}, u32[]{:S(2)}, u32[]{:S(2)}) collective-permute-start(bf16[128,1536]{1,0:T(8,128)(2,1)S(1)} %pad_maximum_fusion.1.refs_0_), channel_id=1, source_target_pairs={{0,8},{8,16},{16,24},{24,0},{1,9},{9,17},{17,25},{25,1},{2,10},{10... | collective-permute-start | bytes 1179656 | tf_op jit(solution)/shard_map/ppermute | solution.py:19
  108.1 21.0 %collective-permute-start.20 = (bf16[128,1536]{1,0:T(8,128)(2,1)S(1)}, bf16[128,1536]{1,0:T(8,128)(2,1)}, u32[]{:S(2)}, u32[]{:S(2)}) collective-permute-start(bf16[128,1536]{1,0:T(8,128)(2,1)S(1)} %pad_maximum_fusion.2.refs_0_), channel_id=1, source_target_pairs={{0,24},{8,0},{16,8},{24,16},{1,25},{9,1},{17,9},{25,17},{2,26},{10... | collective-permute-start | bytes 1179656 | tf_op jit(solution)/shard_map/ppermute | solution.py:19
  108.1 22.3 %collective-permute-start.21 = (bf16[128,1536]{1,0:T(8,128)(2,1)S(1)}, bf16[128,1536]{1,0:T(8,128)(2,1)}, u32[]{:S(2)}, u32[]{:S(2)}) collective-permute-start(bf16[128,1536]{1,0:T(8,128)(2,1)S(1)} %pad_maximum_fusion.2.refs_0_), channel_id=1, source_target_pairs={{0,16},{8,24},{16,0},{24,8},{1,17},{9,25},{17,1},{25,9},{2,18},{10... | collective-permute-start | bytes 1179656 | tf_op jit(solution)/shard_map/ppermute | solution.py:19
  112.8 23.2 %collective-permute-start.22 = (bf16[128,1536]{1,0:T(8,128)(2,1)S(1)}, bf16[128,1536]{1,0:T(8,128)(2,1)}, u32[]{:S(2)}, u32[]{:S(2)}) collective-permute-start(bf16[128,1536]{1,0:T(8,128)(2,1)S(1)} %pad_maximum_fusion.2.refs_0_), channel_id=1, source_target_pairs={{0,8},{8,16},{16,24},{24,0},{1,9},{9,17},{17,25},{25,1},{2,10},{10... | collective-permute-start | bytes 1179656 | tf_op jit(solution)/shard_map/ppermute | solution.py:19
  127.5 28.6 %collective-permute-start.32 = (f32[128,1536]{1,0:T(8,128)}, f32[128,1536]{1,0:T(8,128)S(1)}, u32[]{:S(2)}, u32[]{:S(2)}) collective-permute-start(f32[128,1536]{1,0:T(8,128)} %get-tuple-element.89), channel_id=1, source_target_pairs={{0,3},{1,0},{2,1},{3,2},{4,7},{5,4},{6,5},{7,6},{8,11},{9,8},{10,9... | collective-permute-start | bytes 2359304 | tf_op jit(solution)/shard_map/ppermute | solution.py:24
  128.4 51.3 %collective-permute-start.33 = (f32[128,1536]{1,0:T(8,128)}, f32[128,1536]{1,0:T(8,128)S(1)}, u32[]{:S(2)}, u32[]{:S(2)}) collective-permute-start(f32[128,1536]{1,0:T(8,128)} %get-tuple-element.91), channel_id=1, source_target_pairs={{0,1},{1,2},{2,3},{3,0},{4,5},{5,6},{6,7},{7,4},{8,9},{9,10},{10,1... | collective-permute-start | bytes 2359304 | tf_op jit(solution)/shard_map/ppermute | solution.py:24
  143.8 16.8 %collective-permute-start.30 = (bf16[128,1536]{1,0:T(8,128)(2,1)}, bf16[128,1536]{1,0:T(8,128)(2,1)}, u32[]{:S(2)}, u32[]{:S(2)}) collective-permute-start(bf16[128,1536]{1,0:T(8,128)(2,1)} %slice.126), channel_id=1, source_target_pairs={{0,8},{8,16},{16,24},{24,0},{1,9},{9,17},{17,25},{25,1},{2,10},{10... | collective-permute-start | bytes 1179656 | tf_op jit(solution)/shard_map/ppermute | solution.py:19
  146.1 20.8 %collective-permute-start.31 = (bf16[128,1536]{1,0:T(8,128)(2,1)S(1)}, bf16[128,1536]{1,0:T(8,128)(2,1)}, u32[]{:S(2)}, u32[]{:S(2)}) collective-permute-start(bf16[128,1536]{1,0:T(8,128)(2,1)S(1)} %slice.127), channel_id=1, source_target_pairs={{0,24},{8,0},{16,8},{24,16},{1,25},{9,1},{17,9},{25,17},{2,26},{10... | collective-permute-start | bytes 1179656 | tf_op jit(solution)/shard_map/ppermute | solution.py:19
  146.5 30.3 %collective-permute-start.23 = (f32[128,1536]{1,0:T(8,128)}, f32[128,1536]{1,0:T(8,128)S(1)}, u32[]{:S(2)}, u32[]{:S(2)}) collective-permute-start(f32[128,1536]{1,0:T(8,128)} %get-tuple-element.71), channel_id=1, source_target_pairs={{0,1},{1,2},{2,3},{3,0},{4,5},{5,6},{6,7},{7,4},{8,9},{9,10},{10,1... | collective-permute-start | bytes 2359304 | tf_op jit(solution)/shard_map/ppermute | solution.py:24
  156.1 20.7 %collective-permute-start.24 = (f32[128,1536]{1,0:T(8,128)}, f32[128,1536]{1,0:T(8,128)S(1)}, u32[]{:S(2)}, u32[]{:S(2)}) collective-permute-start(f32[128,1536]{1,0:T(8,128)} %get-tuple-element.72), channel_id=1, source_target_pairs={{0,3},{1,0},{2,1},{3,2},{4,7},{5,4},{6,5},{7,6},{8,11},{9,8},{10,9... | collective-permute-start | bytes 2359304 | tf_op jit(solution)/shard_map/ppermute | solution.py:24
  160.6 19.1 %collective-permute-start.35 = (f32[64,1536]{1,0:T(8,128)}, f32[64,1536]{1,0:T(8,128)}, u32[]{:S(2)}, u32[]{:S(2)}) collective-permute-start(f32[64,1536]{1,0:T(8,128)} %slice_add_fusion), channel_id=1, source_target_pairs={{0,3},{1,0},{2,1},{3,2},{4,7},{5,4},{6,5},{7,6},{8,11},{9,8},{10,9... | collective-permute-start | bytes 1179656 | tf_op jit(solution)/shard_map/ppermute | solution.py:24
  202.4 23.1 %collective-permute-start.41 = (f32[1,1536]{1,0:T(1,128)S(1)}, f32[1,1536]{1,0:T(1,128)S(1)}, u32[]{:S(2)}, u32[]{:S(2)}) collective-permute-start(f32[1,1536]{1,0:T(1,128)S(1)} %broadcast_in_dim.19), channel_id=1, source_target_pairs={{0,2},{1,3},{2,0},{3,1},{4,6},{5,7},{6,4},{7,5},{8,10},{9,11},{10,... | collective-permute-start | bytes 18440 | tf_op jit(solution)/shard_map/ppermute | solution.py:24
  203.4 22.2 %collective-permute-start.42 = (f32[1,1536]{1,0:T(1,128)S(1)}, f32[1,1536]{1,0:T(1,128)S(1)}, u32[]{:S(2)}, u32[]{:S(2)}) collective-permute-start(f32[1,1536]{1,0:T(1,128)S(1)} %broadcast_in_dim.19), channel_id=1, source_target_pairs={{0,1},{1,2},{2,3},{3,0},{4,5},{5,6},{6,7},{7,4},{8,9},{9,10},{10,1... | collective-permute-start | bytes 18440 | tf_op jit(solution)/shard_map/ppermute | solution.py:24
  205.8 19.7 %collective-permute-start.43 = (f32[1,1536]{1,0:T(1,128)S(1)}, f32[1,1536]{1,0:T(1,128)S(1)}, u32[]{:S(2)}, u32[]{:S(2)}) collective-permute-start(f32[1,1536]{1,0:T(1,128)S(1)} %broadcast_in_dim.19), channel_id=1, source_target_pairs={{0,3},{1,0},{2,1},{3,2},{4,7},{5,4},{6,5},{7,6},{8,11},{9,8},{10,9... | collective-permute-start | bytes 18440 | tf_op jit(solution)/shard_map/ppermute | solution.py:24
  206.4 24.9 %collective-permute-start.45 = (bf16[128,1536]{1,0:T(8,128)(2,1)S(1)}, bf16[128,1536]{1,0:T(8,128)(2,1)S(1)}, u32[]{:S(2)}, u32[]{:S(2)}) collective-permute-start(bf16[128,1536]{1,0:T(8,128)(2,1)S(1)} %fusion.16), channel_id=1, source_target_pairs={{32,0},{64,32},{96,64},{33,1},{65,33},{97,65},{34,2},{66,34},{98,6... | collective-permute-start | bytes 1179656 | tf_op jit(solution)/shard_map/ppermute | solution.py:32
  (49 other events, 576.4 us)
